TPU v7x, 32 devices: a whole 2x2x4 slice. The times are simulated.
32 devices in a mesh: dp: 2 (over y), mp: 16 (over z, x, core).
Axes of the slice: x: 2, y: 2, z: 4, core: 2. Of those that a mesh axis runs over, the one named last changes fastest.
Arguments:
- query: bfloat16 [512, 1024], P('dp', 'mp'), may hold values from -0.75 to 0.75
- kv_cache: bfloat16 [1024, 2048], P('dp', 'mp'), may hold values from -4 to 4, as said below
- out_grad: bfloat16 [512, 1024], P('dp', 'mp'), may hold values from -384 to 384
- source_lengths: int32 [2, 8], P('dp'), may hold values from 1 to 128, 512 in all within a row
- target_lengths: int32 [2, 8], P('dp'), may hold values from 1 to 64, 256 in all within a row
- low_rank: bfloat16 [1024, 32], P(('dp', 'mp')), may hold values from -0.125 to 0.125
- adapter_up_matrix: bfloat16 [32, 1024], replicated, may hold values from -0.1875 to 0.1875
Outputs:
- query_grad: bfloat16 [512, 1024], P('dp', 'mp')
- key_gradient: bfloat16 [1024, 1024], P(('dp', 'mp'))
- value_grad: bfloat16 [1024, 1024], P(('dp', 'mp'))
- low_rank_gradient: float32 [1024, 32], P(('dp', 'mp'))
- adapter_up_gradient: float32 [1024, 32], P(('dp', 'mp'))
Inputs may be any that keep to these rules, and one draw needn't show every extreme that they name: `source_lengths`: each row sums to 512; its largest entry is exactly 128. `target_lengths`: each row sums to 256; its largest entry is exactly 64. `kv_cache`: the key columns lie within -0.75 to 0.75.
All inputs are finite; a program needn't handle non-finite values.
Results may differ from a plain program's by a relative error of at most 0.0053.
Values may be sent and summed in bfloat16 or wider, within the bound.
No kernel may reach another device: no remote copies, remote signals or barrier semaphores. Data moves between devices by JAX's collectives and lax.ppermute only.
A program may use at most 64 MiB of HBM per device.

v0:
```python
import math

import jax
import jax.numpy as jnp
from jax import lax
from jax.sharding import PartitionSpec as P

HS = 64


adapter_factor = 2.0


def doc_index(lengths, count):
    ends = jnp.cumsum(lengths)
    position = jnp.arange(count, dtype=jnp.int32)
    return jnp.sum((position[:, None] >= ends[None, :]).astype(jnp.int32), axis=1)


def tile_terms(query_rows, grad_rows, key_rows, value_rows, row_doc, col_doc):
    scores = jnp.einsum("qhd,khd->hqk", query_rows, key_rows, preferred_element_type=jnp.float32)
    allowed = (row_doc[:, None] == col_doc[None, :])[None]
    expo = jnp.where(allowed, jnp.exp(scores), jnp.zeros_like(scores))
    dprob = jnp.einsum("qhd,khd->hqk", grad_rows, value_rows, preferred_element_type=jnp.float32)
    return (expo, dprob)


def tile_grads(query_rows, grad_rows, key_rows, expo, dprob, total_rows, delta_rows):
    prob = expo / total_rows[:, :, None]
    prob_low = prob.astype(jnp.bfloat16)
    dscore = (prob * (dprob - delta_rows[:, :, None])).astype(jnp.bfloat16)
    query_part = jnp.einsum("hqk,khd->qhd", dscore, key_rows, preferred_element_type=jnp.float32)
    key_part = jnp.einsum("hqk,qhd->khd", dscore, query_rows, preferred_element_type=jnp.float32)
    value_part = jnp.einsum("hqk,qhd->khd", prob_low, grad_rows, preferred_element_type=jnp.float32)
    return (query_part, key_part, value_part)


def dense_pass(query_heads, grad_heads, key_heads, value_heads, tgt_doc, src_doc, key_block):
    src_count = key_heads.shape[0]
    tgt_count, head_count = (query_heads.shape[0], query_heads.shape[1])
    block_count = src_count // key_block

    def take_keys(index):
        start = index * key_block
        key_rows = lax.dynamic_slice_in_dim(key_heads, start, key_block, 0)
        value_rows = lax.dynamic_slice_in_dim(value_heads, start, key_block, 0)
        col_doc = lax.dynamic_slice_in_dim(src_doc, start, key_block, 0)
        return (start, key_rows, value_rows, col_doc)

    def first(index, carry):
        total, weighted = carry
        start, key_rows, value_rows, col_doc = take_keys(index)
        expo, dprob = tile_terms(query_heads, grad_heads, key_rows, value_rows, tgt_doc, col_doc)
        return (total + jnp.sum(expo, axis=2), weighted + jnp.sum(expo * dprob, axis=2))

    zeros = jnp.zeros((head_count, tgt_count), jnp.float32)
    total, weighted = lax.fori_loop(0, block_count, first, (zeros, zeros))
    delta = weighted / total

    def second(index, carry):
        query_acc, key_out, value_out = carry
        start, key_rows, value_rows, col_doc = take_keys(index)
        expo, dprob = tile_terms(query_heads, grad_heads, key_rows, value_rows, tgt_doc, col_doc)
        query_part, key_part, value_part = tile_grads(
            query_heads, grad_heads, key_rows, expo, dprob, total, delta
        )
        key_out = lax.dynamic_update_slice_in_dim(key_out, key_part.astype(jnp.bfloat16), start, 0)
        value_out = lax.dynamic_update_slice_in_dim(
            value_out, value_part.astype(jnp.bfloat16), start, 0
        )
        return (query_acc + query_part, key_out, value_out)

    start_carry = (
        jnp.zeros(query_heads.shape, jnp.float32),
        jnp.zeros(key_heads.shape, jnp.bfloat16),
        jnp.zeros(key_heads.shape, jnp.bfloat16),
    )
    return lax.fori_loop(0, block_count, second, start_carry)


def local(query, kv_cache, out_grad, source_lengths, target_lengths, low_rank, adapter_up_matrix):
    tgt_count = query.shape[0]
    src_count = kv_cache.shape[0]
    head_count = query.shape[1] // HS
    local_width = head_count * HS
    query_heads = query.reshape(tgt_count, head_count, HS)
    grad_heads = out_grad.reshape(tgt_count, head_count, HS)
    both_heads = kv_cache.reshape(src_count, head_count, 2, HS)
    key_heads = both_heads[:, :, 0, :]
    value_heads = both_heads[:, :, 1, :]
    tgt_doc = doc_index(target_lengths[0], tgt_count)
    src_doc = doc_index(source_lengths[0], src_count)
    key_block = math.gcd(src_count, 512)
    query_acc, key_out, value_out = dense_pass(
        query_heads, grad_heads, key_heads, value_heads, tgt_doc, src_doc, key_block
    )
    query_grad = query_acc.reshape(tgt_count, local_width).astype(jnp.bfloat16)
    stacked = jnp.stack(
        [key_out.reshape(src_count, local_width), value_out.reshape(src_count, local_width)]
    )
    rank = adapter_up_matrix.shape[0] // 2
    up_key = adapter_up_matrix[:rank]
    up_value = adapter_up_matrix[rank:]
    owned = lax.all_to_all(stacked, "mp", split_axis=1, concat_axis=2, tiled=True)
    key_gradient = owned[0]
    value_grad = owned[1]
    low_rank_gradient = adapter_factor * jnp.concatenate(
        [
            jnp.einsum("tc,rc->tr", key_gradient, up_key, preferred_element_type=jnp.float32),
            jnp.einsum("tc,rc->tr", value_grad, up_value, preferred_element_type=jnp.float32),
        ],
        axis=1,
    )
    z_key = low_rank[:, :rank]
    z_value = low_rank[:, rank:]
    key_adapter_term = jnp.einsum(
        "tc,tr->cr", key_gradient, z_key, preferred_element_type=jnp.float32
    )
    value_adapter_term = jnp.einsum(
        "tc,tr->cr", value_grad, z_value, preferred_element_type=jnp.float32
    )
    adapter_up_gradient = lax.psum_scatter(
        adapter_factor * jnp.concatenate([key_adapter_term, value_adapter_term], axis=1),
        ("dp", "mp"),
        scatter_dimension=0,
        tiled=True,
    )
    return (query_grad, key_gradient, value_grad, low_rank_gradient, adapter_up_gradient)


def solution(mesh):
    in_specs = (
        P("dp", "mp"),
        P("dp", "mp"),
        P("dp", "mp"),
        P("dp", None),
        P("dp", None),
        P(("dp", "mp"), None),
        P(),
    )
    out_specs = (
        P("dp", "mp"),
        P(("dp", "mp"), None),
        P(("dp", "mp"), None),
        P(("dp", "mp"), None),
        P(("dp", "mp"), None),
    )
    return jax.shard_map(local, mesh=mesh, in_specs=in_specs, out_specs=out_specs, check_vma=False)
```

profile of v0, /device:TPU:0, one launch (start us, length us, event | category | flops | bytes accessed | tf_op | source)
XLA Modules:
  0.0 170.0 jit_solution(55579297177114141)
XLA Ops:
  7.2 0.0 copy-start
  7.2 0.0 copy-start.6
  7.2 0.7 copy-done.6
  7.8 0.2 reduce-window.17
  8.0 0.0 copy-start.7
  8.0 0.7 copy-done.7
  8.7 0.2 reduce-window.16
  8.9 0.1 convert_reduce_fusion.1
  9.0 0.1 convert_reduce_fusion
  9.0 0.0 copy-start.4
  9.0 1.0 copy.33
  10.1 0.0 copy-done.4
  10.1 0.2 fusion.4
  10.3 0.0 copy-done
  10.3 0.4 fusion.13
  10.7 0.2 fusion.2
  11.0 0.1 multiply_convert_fusion
  11.1 0.2 fusion.1
  11.3 0.2 copy.34
  11.5 0.9 reshape.136
  12.4 7.4 %all-to-all-start = ((bf16[16,2,2048]{2,1,0:T(2,128)(2,1)}), bf16[16,2,2048]{2,1,0:T(2,128)(2,1)S(1)}, u32[]{:S(2)}, u32[]{:S(2)}) async-start(bf16[16,2,2048]{2,1,0:T(2,128)(2,1)} %reshape.136), calls=%async_computation | async-start | bytes 262144 | tf_op jit(solution)/shard_map/all_to_all | solution.py:104
  19.7 0.0 reduce-scatter.4.cloned.1.call-start
  19.8 0.8 convolution_convert_fusion.2
  20.6 7.1 %all-to-all-done = bf16[16,2,2048]{2,1,0:T(2,128)(2,1)S(1)} async-done(((bf16[16,2,2048]{2,1,0:T(2,128)(2,1)}), bf16[16,2,2048]{2,1,0:T(2,128)(2,1)S(1)}, u32[]{:S(2)}, u32[]{:S(2)}) %all-to-all-start) | async-done | bytes 131104 | tf_op jit(solution)/shard_map/all_to_all | solution.py:104
  27.7 0.2 reshape.137
  28.0 0.1 copy.37
  28.0 0.0 copy-start.3
  28.0 0.1 squeeze.5
  28.2 0.7 copy-done.3
  28.9 0.0 copy-start.1
  28.9 0.0 copy-start.5
  28.9 0.1 fusion.5
  29.0 0.6 copy-done.5
  29.6 0.3 fusion.9
  29.8 0.0 copy-done.1
  29.8 0.1 copy.36
  29.9 0.1 squeeze.4
  30.0 0.0 copy-start.2
  30.0 0.2 fusion.11
  30.3 1.0 copy.40
  31.3 0.0 reduce-scatter.4.cloned.1.call-update
  31.3 0.0 copy-done.2
  31.3 0.1 fusion.7
  31.4 0.7 copy.38
  32.1 131.0 %reduce-scatter.4.cloned.1.call-done = f32[32,32]{1,0:T(8,128)} async-done(((f32[1024,32]{1,0:T(8,128)}), f32[32,32]{1,0:T(8,128)}) %reduce-scatter.4.cloned.1.call-update) | async-done | bytes 4112
  (6 shorter events, 0.1 us)
Async XLA Ops:
  7.2 3.2 %copy-start = (bf16[256,64]{0,1:T(8,128)(2,1)S(1)}, bf16[256,64]{0,1:T(8,128)(2,1)}, u32[]{:S(2)}) copy-start(bf16[256,64]{0,1:T(8,128)(2,1)} %param.7) | copy-start | bytes 98308
  7.2 0.7 copy-start.6
  8.0 0.7 copy-start.7
  9.0 1.0 copy-start.4
  12.4 15.3 %all-to-all-start = ((bf16[16,2,2048]{2,1,0:T(2,128)(2,1)}), bf16[16,2,2048]{2,1,0:T(2,128)(2,1)S(1)}, u32[]{:S(2)}, u32[]{:S(2)}) async-start(bf16[16,2,2048]{2,1,0:T(2,128)(2,1)} %reshape.136), calls=%async_computation | async-start | bytes 262144 | tf_op jit(solution)/shard_map/all_to_all | solution.py:104
  19.7 143.4 %reduce-scatter.4.cloned.1.call-start = ((), (), s32[]{:S(2)}) async-start(), calls=%async_computation.2 | async-start | bytes 540672
  28.0 0.8 copy-start.3
  28.9 1.0 copy-start.1
  28.9 0.7 copy-start.5
  30.0 1.2 copy-start.2
Sparse Core Ops, SparseCore 0:
  31.4 131.6 reduce-scatter.3
where the time goes:
time: 170 us
  waiting for transfers between devices  138 us (81%)
  between operations  14.2 us (8%)
  starting transfers between devices  7.4 us (4%)
  local copies, waits for them, and re-layouts  6.99 us (4%)
  matrix products  2.57 us (2%)
    unnamed x2, waiting for transfers between devices  131 us
    all_to_all x1, starting transfers between devices, local(): lax.all_to_all(stacked, 'mp', split_axis=1, concat_axis=2, tiled=True)  7.36 us
    all_to_all x1, waiting for transfers between devices, local(): lax.all_to_all(stacked, 'mp', split_axis=1, concat_axis=2, tiled=True)  7.07 us
    unnamed x21, local copies, waits for them, and re-layouts  6.38 us
  transfers between devices with their start and end apart: 2, of which 2 were waited for; matrix products, arithmetic and copies ran while one was open for 1% of the time, Pallas kernels for 0%

commit v1 on v0

v1 whole, which is shorter than its diff:
```python
import functools

import jax
import jax.numpy as jnp
from jax import lax
from jax.experimental import pallas as pl
from jax.experimental.pallas import tpu as pltpu
from jax.sharding import PartitionSpec as P

HS = 64

adapter_factor = 2.0


def doc_of(lengths_ref, shape, dim):
    position = lax.broadcasted_iota(jnp.int32, shape, dim)
    doc = jnp.zeros(shape, jnp.int32)
    end = jnp.int32(0)
    for i in range(lengths_ref.shape[1]):
        end = end + lengths_ref[0, i]
        doc = doc + (position >= end).astype(jnp.int32)
    return doc


def attention_kernel(
    source_ref, target_ref, query_ref, grad_ref, kv_ref, query_grad_ref, both_grad_ref
):
    tgt_count = query_ref.shape[1]
    src_count = kv_ref.shape[0]
    both = kv_ref[...]
    query_t = query_ref[...]
    grad_t = grad_ref[...]
    blank = jnp.zeros_like(query_t)
    query_wide = jnp.concatenate([query_t, blank], axis=0)
    grad_wide = jnp.concatenate([blank, grad_t], axis=0)
    scores = jnp.dot(both, query_wide, preferred_element_type=jnp.float32)
    dprob = jnp.dot(both, grad_wide, preferred_element_type=jnp.float32)
    tgt_doc = doc_of(target_ref, (1, tgt_count), 1)
    src_doc = doc_of(source_ref, (src_count, 1), 0)
    expo = jnp.where(src_doc == tgt_doc, jnp.exp(scores), 0.0)
    total = jnp.sum(expo, axis=0, keepdims=True)
    delta = jnp.sum(expo * dprob, axis=0, keepdims=True) / total
    prob = expo / total
    prob_low = prob.astype(jnp.bfloat16)
    dscore = (prob * (dprob - delta)).astype(jnp.bfloat16)
    nt = (((1,), (1,)), ((), ()))
    both_grad = lax.dot_general(dscore, query_wide, nt, preferred_element_type=jnp.float32)
    both_grad += lax.dot_general(prob_low, grad_wide, nt, preferred_element_type=jnp.float32)
    both_grad_ref[...] = both_grad.astype(jnp.bfloat16)
    tn = (((0,), (0,)), ((), ()))
    query_grad = lax.dot_general(both, dscore, tn, preferred_element_type=jnp.float32)
    query_grad_ref[...] = query_grad[:HS].astype(jnp.bfloat16)


def adapter_kernel(parts, both_grad_ref, *refs):
    low_refs = refs[:parts]
    out_refs = refs[parts:-1]
    low = refs[-1]
    me = lax.axis_index("mp")
    rows = low_refs[0].shape[0]
    for shift in range(parts):
        owner = lax.rem(me + parts - shift, parts)
        low[pl.ds(pl.multiple_of(owner * rows, rows), rows), :] = low_refs[shift][...]
    tn = (((0,), (0,)), ((), ()))
    share = adapter_factor * lax.dot_general(
        both_grad_ref[...], low[...], tn, preferred_element_type=jnp.float32
    )
    column = lax.broadcasted_iota(jnp.int32, (HS, share.shape[1]), 1)
    share = jnp.where(column < share.shape[1] // 2, share[:HS], share[HS:])
    step = HS // len(out_refs)
    for j, out_ref in enumerate(out_refs):
        out_ref[...] = share[j * step:(j + 1) * step]


def owner_kernel(heads, got_ref, up_ref, *refs):
    share_refs = refs[:-4]
    key_ref, value_ref, low_grad_ref, up_grad_ref = refs[-4:]
    rows = key_ref.shape[0]
    rank = up_ref.shape[0] // 2
    for pair in range(heads // 2):
        first = got_ref[2 * pair * rows:(2 * pair + 1) * rows, :]
        second = got_ref[(2 * pair + 1) * rows:(2 * pair + 2) * rows, :]
        columns = slice(2 * pair * HS, (2 * pair + 2) * HS)
        key_ref[:, columns] = jnp.concatenate([first[:, :HS], second[:, :HS]], axis=1)
        value_ref[:, columns] = jnp.concatenate([first[:, HS:], second[:, HS:]], axis=1)
    nt = (((1,), (1,)), ((), ()))
    up = up_ref[...]
    from_key = lax.dot_general(key_ref[...], up, nt, preferred_element_type=jnp.float32)
    from_value = lax.dot_general(value_ref[...], up, nt, preferred_element_type=jnp.float32)
    column = lax.broadcasted_iota(jnp.int32, from_key.shape, 1)
    low_grad_ref[...] = adapter_factor * jnp.where(column < rank, from_key, from_value)
    total = share_refs[0][...]
    for share_ref in share_refs[1:]:
        total = total + share_ref[...]
    up_grad_ref[...] = total


def local(dp, mp, query, kv_cache, out_grad, source_lengths, target_lengths, low_rank, adapter_up_matrix):
    tgt_count = query.shape[0]
    src_count = kv_cache.shape[0]
    rows = low_rank.shape[0]
    both_rank = low_rank.shape[1]
    width = adapter_up_matrix.shape[1]
    vmem = pl.BlockSpec(memory_space=pltpu.VMEM)
    smem = pl.BlockSpec(memory_space=pltpu.SMEM)
    params = pltpu.CompilerParams(vmem_limit_bytes=48 * 1024 * 1024)

    lows = [low_rank]
    for shift in range(1, mp):
        lows.append(lax.ppermute(low_rank, "mp", [(m, (m + shift) % mp) for m in range(mp)]))

    query_grad_t, both_grad = pl.pallas_call(
        attention_kernel,
        out_shape=[
            jax.ShapeDtypeStruct((HS, tgt_count), jnp.bfloat16),
            jax.ShapeDtypeStruct((src_count, 2 * HS), jnp.bfloat16),
        ],
        in_specs=[smem, smem, vmem, vmem, vmem],
        out_specs=[vmem, vmem],
        compiler_params=params,
        name="attention_backward",
    )(source_lengths, target_lengths, query.T, out_grad.T, kv_cache)

    got = lax.all_to_all(both_grad, "mp", split_axis=0, concat_axis=0, tiled=True)

    share_rows = HS // dp
    shares = pl.pallas_call(
        functools.partial(adapter_kernel, mp),
        out_shape=[jax.ShapeDtypeStruct((share_rows, both_rank), jnp.float32)] * dp,
        in_specs=[vmem] * (1 + mp),
        out_specs=[vmem] * dp,
        scratch_shapes=[pltpu.VMEM((mp * rows, both_rank), jnp.bfloat16)],
        compiler_params=params,
        name="adapter_shares",
    )(both_grad, *lows)

    mine = lax.axis_index("dp")
    arrived = []
    for step in range(dp):
        turn = (mine + step) % dp
        sent = shares[0]
        for j in range(1, dp):
            sent = jnp.where(turn == j, shares[j], sent)
        route = [(d * mp + h, h * dp + (d + step) % dp) for d in range(dp) for h in range(mp)]
        arrived.append(lax.ppermute(sent, ("dp", "mp"), route))

    key_gradient, value_grad, low_grad, up_grad = pl.pallas_call(
        functools.partial(owner_kernel, mp),
        out_shape=[
            jax.ShapeDtypeStruct((rows, width), jnp.bfloat16),
            jax.ShapeDtypeStruct((rows, width), jnp.bfloat16),
            jax.ShapeDtypeStruct((rows, both_rank), jnp.float32),
            jax.ShapeDtypeStruct((share_rows, both_rank), jnp.float32),
        ],
        in_specs=[vmem] * (2 + dp),
        out_specs=[vmem] * 4,
        compiler_params=params,
        name="owner_outputs",
    )(got, adapter_up_matrix, *arrived)
    return query_grad_t.T, key_gradient, value_grad, low_grad, up_grad


def solution(mesh):
    in_specs = (
        P("dp", "mp"),
        P("dp", "mp"),
        P("dp", "mp"),
        P("dp", None),
        P("dp", None),
        P(("dp", "mp"), None),
        P(),
    )
    out_specs = (
        P("dp", "mp"),
        P(("dp", "mp"), None),
        P(("dp", "mp"), None),
        P(("dp", "mp"), None),
        P(("dp", "mp"), None),
    )
    body = functools.partial(local, mesh.shape["dp"], mesh.shape["mp"])
    return jax.shard_map(body, mesh=mesh, in_specs=in_specs, out_specs=out_specs, check_vma=False)
```

time: 170 us -> 48.9 us (0.29)
  the two profiles are of different devices: /device:TPU:0 before, /device:TPU:25 now
where the time goes in v1:
time: 48.9 us; the launch traced here: 48.5 us
  starting transfers between devices  31.6 us (65%)
  waiting for transfers between devices  8.99 us (18%)
  Pallas kernels  4.09 us (8%)
  local copies, waits for them, and re-layouts  3.08 us (6%)
  between operations  0.73 us (1%)
    ppermute x15, starting transfers between devices, local(): lax.ppermute(low_rank, 'mp', [(m, (m + shift) % mp) for m in range(mp)])  21.3 us
    all_to_all x1, starting transfers between devices, local(): lax.all_to_all(both_grad, 'mp', split_axis=0, concat_axis=0, tiled=True)  6.49 us
    ppermute x2, waiting for transfers between devices, local(): arrived.append(lax.ppermute(sent, ('dp', 'mp'), route))  5.9 us
    ppermute x2, starting transfers between devices, local(): arrived.append(lax.ppermute(sent, ('dp', 'mp'), route))  3.83 us
    unnamed x14, local copies, waits for them, and re-layouts  3.08 us
    ppermute x15, waiting for transfers between devices, local(): lax.ppermute(low_rank, 'mp', [(m, (m + shift) % mp) for m in range(mp)])  3.08 us
    pallas_call x1, Pallas kernels, local(): pl.pallas_call(attention_kernel, out_shape=[jax.ShapeDtypeStruct((HS, tgt...  2.1 us
    pallas_call x1, Pallas kernels, local(): pl.pallas_call(functools.partial(adapter_kernel, mp), out_shape=[jax.Shap...  1.13 us
  transfers between devices with their start and end apart: 18, of which 4 were waited for; matrix products, arithmetic and copies ran while one was open for 0% of the time, Pallas kernels for 2%

profile of v1, /device:TPU:25, one launch (start us, length us, event | category | flops | bytes accessed | tf_op | source)
XLA Modules:
  0.0 48.5 jit_solution(16370642519474094200)
XLA Ops:
  0.6 0.0 copy-start.5
  0.6 0.0 copy-start.6
  0.7 0.6 %copy-done.5 = s32[1,8]{1,0:T(1,128)S(1)} copy-done((s32[1,8]{1,0:T(1,128)S(1)}, s32[1,8]{1,0:T(1,128)}, u32[]{:S(2)}) %copy-start.5) | copy-done | bytes 56
  1.3 0.0 copy-done.6
  1.3 0.0 copy-start
  1.3 0.9 %copy-done = bf16[512,128]{1,0:T(8,128)(2,1)S(1)} copy-done((bf16[512,128]{1,0:T(8,128)(2,1)S(1)}, bf16[512,128]{1,0:T(8,128)(2,1)}, u32[]{:S(2)}) %copy-start) | copy-done | bytes 131096
  2.2 0.0 copy-start.2
  2.2 0.8 %copy-done.2 = bf16[256,64]{0,1:T(8,128)(2,1)S(1)} copy-done((bf16[256,64]{0,1:T(8,128)(2,1)S(1)}, bf16[256,64]{0,1:T(8,128)(2,1)}, u32[]{:S(2)}) %copy-start.2) | copy-done | bytes 32792
  3.0 0.0 copy-start.3
  3.0 0.8 %copy-done.3 = bf16[256,64]{0,1:T(8,128)(2,1)S(1)} copy-done((bf16[256,64]{0,1:T(8,128)(2,1)S(1)}, bf16[256,64]{0,1:T(8,128)(2,1)}, u32[]{:S(2)}) %copy-start.3) | copy-done | bytes 32792
  3.7 2.1 %attention_backward.1 = (bf16[64,256]{1,0:T(8,128)(2,1)}, bf16[512,128]{1,0:T(8,128)(2,1)}) custom-call(s32[1,8]{1,0:T(1,128)S(1)} %copy-done.5, s32[1,8]{1,0:T(1,128)S(1)} %copy-done.6, bf16[64,256]{1,0:T(8,128)(2,1)S(1)} %bitcast.6, bf16[64,256]{1,0:T(8,128)(2,1)S(1)} %bitcast.7, bf16[512,128]{1,0:T(8,128)(2,1)S(1)} %copy-done), custom_call_target="tpu_custom_call" | custom-call | tf_op jit(solution)/shard_map/attention_backward/pallas_call | solution.py:112
  5.8 0.0 copy-start.4
  5.8 6.5 %all-to-all-start = ((bf16[16,32,128]{2,1,0:T(8,128)(2,1)}), bf16[16,32,128]{2,1,0:T(8,128)(2,1)S(1)}, u32[]{:S(2)}, u32[]{:S(2)}) async-start(bf16[16,32,128]{2,1,0:T(8,128)(2,1)} %bitcast.3), calls=%async_computation | async-start | bytes 262144 | tf_op jit(solution)/shard_map/all_to_all | solution.py:124
  12.3 0.0 copy-done.4
  12.3 1.2 %collective-permute-start.13 = (bf16[32,32]{1,0:T(8,128)(2,1)S(1)}, bf16[32,32]{1,0:T(8,128)(2,1)S(1)}, u32[]{:S(2)}, u32[]{:S(2)}) collective-permute-start(bf16[32,32]{1,0:T(8,128)(2,1)S(1)} %copy-done.4), channel_id=1, source_target_pairs={{0,14},{1,15},{2,0},{3,1},{4,2},{5,3},{6,4},{7,5},{8,6},{9,7},{10,... | collective-permute-start | bytes 6152 | tf_op jit(solution)/shard_map/ppermute | solution.py:110
  13.6 0.8 %collective-permute-start.12 = (bf16[32,32]{1,0:T(8,128)(2,1)S(1)}, bf16[32,32]{1,0:T(8,128)(2,1)S(1)}, u32[]{:S(2)}, u32[]{:S(2)}) collective-permute-start(bf16[32,32]{1,0:T(8,128)(2,1)S(1)} %copy-done.4), channel_id=1, source_target_pairs={{0,13},{1,14},{2,15},{3,0},{4,1},{5,2},{6,3},{7,4},{8,5},{9,6},{10... | collective-permute-start | bytes 6152 | tf_op jit(solution)/shard_map/ppermute | solution.py:110
  14.4 0.3 collective-permute-start.11
  14.6 3.0 %collective-permute-start.10 = (bf16[32,32]{1,0:T(8,128)(2,1)S(1)}, bf16[32,32]{1,0:T(8,128)(2,1)S(1)}, u32[]{:S(2)}, u32[]{:S(2)}) collective-permute-start(bf16[32,32]{1,0:T(8,128)(2,1)S(1)} %copy-done.4), channel_id=1, source_target_pairs={{0,11},{1,12},{2,13},{3,14},{4,15},{5,0},{6,1},{7,2},{8,3},{9,4},{... | collective-permute-start | bytes 6152 | tf_op jit(solution)/shard_map/ppermute | solution.py:110
  17.7 0.9 %collective-permute-start.9 = (bf16[32,32]{1,0:T(8,128)(2,1)S(1)}, bf16[32,32]{1,0:T(8,128)(2,1)S(1)}, u32[]{:S(2)}, u32[]{:S(2)}) collective-permute-start(bf16[32,32]{1,0:T(8,128)(2,1)S(1)} %copy-done.4), channel_id=1, source_target_pairs={{0,10},{1,11},{2,12},{3,13},{4,14},{5,15},{6,0},{7,1},{8,2},{9,3},... | collective-permute-start | bytes 6152 | tf_op jit(solution)/shard_map/ppermute | solution.py:110
  18.6 0.0 collective-permute-done.13.refs_14_
  18.6 1.1 %collective-permute-start.8 = (bf16[32,32]{1,0:T(8,128)(2,1)S(1)}, bf16[32,32]{1,0:T(8,128)(2,1)S(1)}, u32[]{:S(2)}, u32[]{:S(2)}) collective-permute-start(bf16[32,32]{1,0:T(8,128)(2,1)S(1)} %copy-done.4), channel_id=1, source_target_pairs={{0,9},{1,10},{2,11},{3,12},{4,13},{5,14},{6,15},{7,0},{8,1},{9,2},... | collective-permute-start | bytes 6152 | tf_op jit(solution)/shard_map/ppermute | solution.py:110
  19.7 0.0 collective-permute-done.12.refs_13_
  19.7 3.0 %collective-permute-start.7 = (bf16[32,32]{1,0:T(8,128)(2,1)S(1)}, bf16[32,32]{1,0:T(8,128)(2,1)S(1)}, u32[]{:S(2)}, u32[]{:S(2)}) collective-permute-start(bf16[32,32]{1,0:T(8,128)(2,1)S(1)} %copy-done.4), channel_id=1, source_target_pairs={{0,8},{1,9},{2,10},{3,11},{4,12},{5,13},{6,14},{7,15},{8,0},{9,1},... | collective-permute-start | bytes 6152 | tf_op jit(solution)/shard_map/ppermute | solution.py:110
  22.6 0.0 collective-permute-done.11.refs_12_
  22.6 0.0 collective-permute-start.6
  22.6 0.0 collective-permute-done.10.refs_11_
  22.7 3.3 %collective-permute-start.5 = (bf16[32,32]{1,0:T(8,128)(2,1)S(1)}, bf16[32,32]{1,0:T(8,128)(2,1)S(1)}, u32[]{:S(2)}, u32[]{:S(2)}) collective-permute-start(bf16[32,32]{1,0:T(8,128)(2,1)S(1)} %copy-done.4), channel_id=1, source_target_pairs={{0,6},{1,7},{2,8},{3,9},{4,10},{5,11},{6,12},{7,13},{8,14},{9,15},... | collective-permute-start | bytes 6152 | tf_op jit(solution)/shard_map/ppermute | solution.py:110
  26.0 0.0 collective-permute-done.9.refs_10_
  26.0 1.7 %collective-permute-start.4 = (bf16[32,32]{1,0:T(8,128)(2,1)S(1)}, bf16[32,32]{1,0:T(8,128)(2,1)S(1)}, u32[]{:S(2)}, u32[]{:S(2)}) collective-permute-start(bf16[32,32]{1,0:T(8,128)(2,1)S(1)} %copy-done.4), channel_id=1, source_target_pairs={{0,5},{1,6},{2,7},{3,8},{4,9},{5,10},{6,11},{7,12},{8,13},{9,14},{... | collective-permute-start | bytes 6152 | tf_op jit(solution)/shard_map/ppermute | solution.py:110
  27.7 0.0 collective-permute-done.8.refs_9_
  27.7 1.0 %collective-permute-start.3 = (bf16[32,32]{1,0:T(8,128)(2,1)S(1)}, bf16[32,32]{1,0:T(8,128)(2,1)S(1)}, u32[]{:S(2)}, u32[]{:S(2)}) collective-permute-start(bf16[32,32]{1,0:T(8,128)(2,1)S(1)} %copy-done.4), channel_id=1, source_target_pairs={{0,4},{1,5},{2,6},{3,7},{4,8},{5,9},{6,10},{7,11},{8,12},{9,13},{1... | collective-permute-start | bytes 6152 | tf_op jit(solution)/shard_map/ppermute | solution.py:110
  28.6 0.0 collective-permute-done.7.refs_8_
  28.6 1.5 %collective-permute-start.2 = (bf16[32,32]{1,0:T(8,128)(2,1)S(1)}, bf16[32,32]{1,0:T(8,128)(2,1)S(1)}, u32[]{:S(2)}, u32[]{:S(2)}) collective-permute-start(bf16[32,32]{1,0:T(8,128)(2,1)S(1)} %copy-done.4), channel_id=1, source_target_pairs={{0,3},{1,4},{2,5},{3,6},{4,7},{5,8},{6,9},{7,10},{8,11},{9,12},{10... | collective-permute-start | bytes 6152 | tf_op jit(solution)/shard_map/ppermute | solution.py:110
  30.1 0.0 collective-permute-done.6.refs_7_
  30.1 0.0 collective-permute-start.1
  30.1 0.0 collective-permute-done.5.refs_6_
  30.1 3.5 %collective-permute-start = (bf16[32,32]{1,0:T(8,128)(2,1)S(1)}, bf16[32,32]{1,0:T(8,128)(2,1)S(1)}, u32[]{:S(2)}, u32[]{:S(2)}) collective-permute-start(bf16[32,32]{1,0:T(8,128)(2,1)S(1)} %copy-done.4), channel_id=1, source_target_pairs={{0,1},{1,2},{2,3},{3,4},{4,5},{5,6},{6,7},{7,8},{8,9},{9,10},{10,1... | collective-permute-start | bytes 6152 | tf_op jit(solution)/shard_map/ppermute | solution.py:110
  33.6 0.0 collective-permute-done.4.refs_5_
  33.6 0.0 collective-permute-start.14
  33.6 0.0 collective-permute-done.3.refs_4_
  33.7 0.0 collective-permute-done.2.refs_3_
  33.7 0.0 collective-permute-done.1.refs_2_
  33.7 0.8 %collective-permute-done.refs_1_ = bf16[32,32]{1,0:T(8,128)(2,1)S(1)} collective-permute-done((bf16[32,32]{1,0:T(8,128)(2,1)S(1)}, bf16[32,32]{1,0:T(8,128)(2,1)S(1)}, u32[]{:S(2)}, u32[]{:S(2)}) %collective-permute-start) | collective-permute-done | bytes 2080 | tf_op jit(solution)/shard_map/ppermute | solution.py:110
  34.4 2.3 %collective-permute-done.14.refs_15_ = bf16[32,32]{1,0:T(8,128)(2,1)S(1)} collective-permute-done((bf16[32,32]{1,0:T(8,128)(2,1)S(1)}, bf16[32,32]{1,0:T(8,128)(2,1)S(1)}, u32[]{:S(2)}, u32[]{:S(2)}) %collective-permute-start.14) | collective-permute-done | bytes 2080 | tf_op jit(solution)/shard_map/ppermute | solution.py:110
  36.7 1.1 %adapter_shares.1 = (f32[32,32]{1,0:T(8,128)S(1)}, f32[32,32]{1,0:T(8,128)S(1)}) custom-call(bf16[512,128]{1,0:T(8,128)(2,1)} %get-tuple-element.14.both_grad_ref, bf16[32,32]{1,0:T(8,128)(2,1)S(1)} %copy-done.4, bf16[32,32]{1,0:T(8,128)(2,1)S(1)} %collective-permute-done.refs_1_, bf16[32,32]{1,0:T(8,128)(2,1)S(1)} %collective-permute-done.1.refs_2_, ...), custom_call_target="tpu_custom_call" | custom-call | tf_op jit(solution)/shard_map/adapter_shares/pallas_call | solution.py:127
  37.9 0.0 copy-start.1
  37.9 1.9 %collective-permute-start.16 = (f32[32,32]{1,0:T(8,128)S(1)}, f32[32,32]{1,0:T(8,128)S(1)}, u32[]{:S(2)}, u32[]{:S(2)}) collective-permute-start(f32[32,32]{1,0:T(8,128)S(1)} %get-tuple-element.21), channel_id=1, source_target_pairs={{0,1},{1,3},{2,5},{3,7},{4,9},{5,11},{6,13},{7,15},{8,17},{9,19},{... | collective-permute-start | bytes 12296 | tf_op jit(solution)/shard_map/ppermute | solution.py:145
  39.8 1.9 %collective-permute-start.15 = (f32[32,32]{1,0:T(8,128)S(1)}, f32[32,32]{1,0:T(8,128)S(1)}, u32[]{:S(2)}, u32[]{:S(2)}) collective-permute-start(f32[32,32]{1,0:T(8,128)S(1)} %get-tuple-element.22), channel_id=1, source_target_pairs={{0,0},{1,2},{2,4},{3,6},{4,8},{5,10},{6,12},{7,14},{8,16},{9,18},{... | collective-permute-start | bytes 12296 | tf_op jit(solution)/shard_map/ppermute | solution.py:145
  41.7 1.2 %collective-permute-done.16.refs_1_ = f32[32,32]{1,0:T(8,128)S(1)} collective-permute-done((f32[32,32]{1,0:T(8,128)S(1)}, f32[32,32]{1,0:T(8,128)S(1)}, u32[]{:S(2)}, u32[]{:S(2)}) %collective-permute-start.16) | collective-permute-done | bytes 4128 | tf_op jit(solution)/shard_map/ppermute | solution.py:145
  42.9 4.7 %collective-permute-done.15.refs_0_ = f32[32,32]{1,0:T(8,128)S(1)} collective-permute-done((f32[32,32]{1,0:T(8,128)S(1)}, f32[32,32]{1,0:T(8,128)S(1)}, u32[]{:S(2)}, u32[]{:S(2)}) %collective-permute-start.15) | collective-permute-done | bytes 4128 | tf_op jit(solution)/shard_map/ppermute | solution.py:145
  47.6 0.0 all-to-all-done
  47.6 0.0 copy-done.1
  47.6 0.9 %owner_outputs.1 = (bf16[32,1024]{1,0:T(8,128)(2,1)}, bf16[32,1024]{1,0:T(8,128)(2,1)}, f32[32,32]{1,0:T(8,128)}, f32[32,32]{1,0:T(8,128)}) custom-call(bf16[512,128]{1,0:T(8,128)(2,1)S(1)} %bitcast.5, bf16[32,1024]{1,0:T(8,128)(2,1)S(1)} %copy-done.1, f32[32,32]{1,0:T(8,128)S(1)} %collective-permute-done.15.refs_0_, ...), custom_call_target="tpu_custom_call" | custom-call | tf_op jit(solution)/shard_map/owner_outputs/pallas_call | solution.py:147
  (1 shorter events, 0.0 us)
Async XLA Ops:
  0.6 0.7 %copy-start.5 = (s32[1,8]{1,0:T(1,128)S(1)}, s32[1,8]{1,0:T(1,128)}, u32[]{:S(2)}) copy-start(s32[1,8]{1,0:T(1,128)} %source_ref.1) | copy-start | bytes 100
  0.6 0.7 %copy-start.6 = (s32[1,8]{1,0:T(1,128)S(1)}, s32[1,8]{1,0:T(1,128)}, u32[]{:S(2)}) copy-start(s32[1,8]{1,0:T(1,128)} %target_ref.1) | copy-start | bytes 100
  1.3 0.9 %copy-start = (bf16[512,128]{1,0:T(8,128)(2,1)S(1)}, bf16[512,128]{1,0:T(8,128)(2,1)}, u32[]{:S(2)}) copy-start(bf16[512,128]{1,0:T(8,128)(2,1)} %kv_ref.1) | copy-start | bytes 393220
  2.2 0.8 %copy-start.2 = (bf16[256,64]{0,1:T(8,128)(2,1)S(1)}, bf16[256,64]{0,1:T(8,128)(2,1)}, u32[]{:S(2)}) copy-start(bf16[256,64]{0,1:T(8,128)(2,1)} %param.7) | copy-start | bytes 98308
  3.0 0.8 %copy-start.3 = (bf16[256,64]{0,1:T(8,128)(2,1)S(1)}, bf16[256,64]{0,1:T(8,128)(2,1)}, u32[]{:S(2)}) copy-start(bf16[256,64]{0,1:T(8,128)(2,1)} %param.9) | copy-start | bytes 98308
  5.8 6.5 %copy-start.4 = (bf16[32,32]{1,0:T(8,128)(2,1)S(1)}, bf16[32,32]{1,0:T(8,128)(2,1)}, u32[]{:S(2)}) copy-start(bf16[32,32]{1,0:T(8,128)(2,1)} %refs_0_.1) | copy-start | bytes 6148
  5.8 41.8 %all-to-all-start = ((bf16[16,32,128]{2,1,0:T(8,128)(2,1)}), bf16[16,32,128]{2,1,0:T(8,128)(2,1)S(1)}, u32[]{:S(2)}, u32[]{:S(2)}) async-start(bf16[16,32,128]{2,1,0:T(8,128)(2,1)} %bitcast.3), calls=%async_computation | async-start | bytes 262144 | tf_op jit(solution)/shard_map/all_to_all | solution.py:124
  12.3 6.2 %collective-permute-start.13 = (bf16[32,32]{1,0:T(8,128)(2,1)S(1)}, bf16[32,32]{1,0:T(8,128)(2,1)S(1)}, u32[]{:S(2)}, u32[]{:S(2)}) collective-permute-start(bf16[32,32]{1,0:T(8,128)(2,1)S(1)} %copy-done.4), channel_id=1, source_target_pairs={{0,14},{1,15},{2,0},{3,1},{4,2},{5,3},{6,4},{7,5},{8,6},{9,7},{10,... | collective-permute-start | bytes 6152 | tf_op jit(solution)/shard_map/ppermute | solution.py:110
  13.6 6.1 %collective-permute-start.12 = (bf16[32,32]{1,0:T(8,128)(2,1)S(1)}, bf16[32,32]{1,0:T(8,128)(2,1)S(1)}, u32[]{:S(2)}, u32[]{:S(2)}) collective-permute-start(bf16[32,32]{1,0:T(8,128)(2,1)S(1)} %copy-done.4), channel_id=1, source_target_pairs={{0,13},{1,14},{2,15},{3,0},{4,1},{5,2},{6,3},{7,4},{8,5},{9,6},{10... | collective-permute-start | bytes 6152 | tf_op jit(solution)/shard_map/ppermute | solution.py:110
  14.4 8.3 %collective-permute-start.11 = (bf16[32,32]{1,0:T(8,128)(2,1)S(1)}, bf16[32,32]{1,0:T(8,128)(2,1)S(1)}, u32[]{:S(2)}, u32[]{:S(2)}) collective-permute-start(bf16[32,32]{1,0:T(8,128)(2,1)S(1)} %copy-done.4), channel_id=1, source_target_pairs={{0,12},{1,13},{2,14},{3,15},{4,0},{5,1},{6,2},{7,3},{8,4},{9,5},{1... | collective-permute-start | bytes 6152 | tf_op jit(solution)/shard_map/ppermute | solution.py:110
  14.6 8.0 %collective-permute-start.10 = (bf16[32,32]{1,0:T(8,128)(2,1)S(1)}, bf16[32,32]{1,0:T(8,128)(2,1)S(1)}, u32[]{:S(2)}, u32[]{:S(2)}) collective-permute-start(bf16[32,32]{1,0:T(8,128)(2,1)S(1)} %copy-done.4), channel_id=1, source_target_pairs={{0,11},{1,12},{2,13},{3,14},{4,15},{5,0},{6,1},{7,2},{8,3},{9,4},{... | collective-permute-start | bytes 6152 | tf_op jit(solution)/shard_map/ppermute | solution.py:110
  17.7 8.3 %collective-permute-start.9 = (bf16[32,32]{1,0:T(8,128)(2,1)S(1)}, bf16[32,32]{1,0:T(8,128)(2,1)S(1)}, u32[]{:S(2)}, u32[]{:S(2)}) collective-permute-start(bf16[32,32]{1,0:T(8,128)(2,1)S(1)} %copy-done.4), channel_id=1, source_target_pairs={{0,10},{1,11},{2,12},{3,13},{4,14},{5,15},{6,0},{7,1},{8,2},{9,3},... | collective-permute-start | bytes 6152 | tf_op jit(solution)/shard_map/ppermute | solution.py:110
  18.6 9.1 %collective-permute-start.8 = (bf16[32,32]{1,0:T(8,128)(2,1)S(1)}, bf16[32,32]{1,0:T(8,128)(2,1)S(1)}, u32[]{:S(2)}, u32[]{:S(2)}) collective-permute-start(bf16[32,32]{1,0:T(8,128)(2,1)S(1)} %copy-done.4), channel_id=1, source_target_pairs={{0,9},{1,10},{2,11},{3,12},{4,13},{5,14},{6,15},{7,0},{8,1},{9,2},... | collective-permute-start | bytes 6152 | tf_op jit(solution)/shard_map/ppermute | solution.py:110
  19.7 9.0 %collective-permute-start.7 = (bf16[32,32]{1,0:T(8,128)(2,1)S(1)}, bf16[32,32]{1,0:T(8,128)(2,1)S(1)}, u32[]{:S(2)}, u32[]{:S(2)}) collective-permute-start(bf16[32,32]{1,0:T(8,128)(2,1)S(1)} %copy-done.4), channel_id=1, source_target_pairs={{0,8},{1,9},{2,10},{3,11},{4,12},{5,13},{6,14},{7,15},{8,0},{9,1},... | collective-permute-start | bytes 6152 | tf_op jit(solution)/shard_map/ppermute | solution.py:110
  22.6 7.4 %collective-permute-start.6 = (bf16[32,32]{1,0:T(8,128)(2,1)S(1)}, bf16[32,32]{1,0:T(8,128)(2,1)S(1)}, u32[]{:S(2)}, u32[]{:S(2)}) collective-permute-start(bf16[32,32]{1,0:T(8,128)(2,1)S(1)} %copy-done.4), channel_id=1, source_target_pairs={{0,7},{1,8},{2,9},{3,10},{4,11},{5,12},{6,13},{7,14},{8,15},{9,0},... | collective-permute-start | bytes 6152 | tf_op jit(solution)/shard_map/ppermute | solution.py:110
  22.7 7.4 %collective-permute-start.5 = (bf16[32,32]{1,0:T(8,128)(2,1)S(1)}, bf16[32,32]{1,0:T(8,128)(2,1)S(1)}, u32[]{:S(2)}, u32[]{:S(2)}) collective-permute-start(bf16[32,32]{1,0:T(8,128)(2,1)S(1)} %copy-done.4), channel_id=1, source_target_pairs={{0,6},{1,7},{2,8},{3,9},{4,10},{5,11},{6,12},{7,13},{8,14},{9,15},... | collective-permute-start | bytes 6152 | tf_op jit(solution)/shard_map/ppermute | solution.py:110
  26.0 7.7 %collective-permute-start.4 = (bf16[32,32]{1,0:T(8,128)(2,1)S(1)}, bf16[32,32]{1,0:T(8,128)(2,1)S(1)}, u32[]{:S(2)}, u32[]{:S(2)}) collective-permute-start(bf16[32,32]{1,0:T(8,128)(2,1)S(1)} %copy-done.4), channel_id=1, source_target_pairs={{0,5},{1,6},{2,7},{3,8},{4,9},{5,10},{6,11},{7,12},{8,13},{9,14},{... | collective-permute-start | bytes 6152 | tf_op jit(solution)/shard_map/ppermute | solution.py:110
  27.7 6.0 %collective-permute-start.3 = (bf16[32,32]{1,0:T(8,128)(2,1)S(1)}, bf16[32,32]{1,0:T(8,128)(2,1)S(1)}, u32[]{:S(2)}, u32[]{:S(2)}) collective-permute-start(bf16[32,32]{1,0:T(8,128)(2,1)S(1)} %copy-done.4), channel_id=1, source_target_pairs={{0,4},{1,5},{2,6},{3,7},{4,8},{5,9},{6,10},{7,11},{8,12},{9,13},{1... | collective-permute-start | bytes 6152 | tf_op jit(solution)/shard_map/ppermute | solution.py:110
  28.6 5.0 %collective-permute-start.2 = (bf16[32,32]{1,0:T(8,128)(2,1)S(1)}, bf16[32,32]{1,0:T(8,128)(2,1)S(1)}, u32[]{:S(2)}, u32[]{:S(2)}) collective-permute-start(bf16[32,32]{1,0:T(8,128)(2,1)S(1)} %copy-done.4), channel_id=1, source_target_pairs={{0,3},{1,4},{2,5},{3,6},{4,7},{5,8},{6,9},{7,10},{8,11},{9,12},{10... | collective-permute-start | bytes 6152 | tf_op jit(solution)/shard_map/ppermute | solution.py:110
  30.1 3.6 %collective-permute-start.1 = (bf16[32,32]{1,0:T(8,128)(2,1)S(1)}, bf16[32,32]{1,0:T(8,128)(2,1)S(1)}, u32[]{:S(2)}, u32[]{:S(2)}) collective-permute-start(bf16[32,32]{1,0:T(8,128)(2,1)S(1)} %copy-done.4), channel_id=1, source_target_pairs={{0,2},{1,3},{2,4},{3,5},{4,6},{5,7},{6,8},{7,9},{8,10},{9,11},{10,... | collective-permute-start | bytes 6152 | tf_op jit(solution)/shard_map/ppermute | solution.py:110
  30.1 4.3 %collective-permute-start = (bf16[32,32]{1,0:T(8,128)(2,1)S(1)}, bf16[32,32]{1,0:T(8,128)(2,1)S(1)}, u32[]{:S(2)}, u32[]{:S(2)}) collective-permute-start(bf16[32,32]{1,0:T(8,128)(2,1)S(1)} %copy-done.4), channel_id=1, source_target_pairs={{0,1},{1,2},{2,3},{3,4},{4,5},{5,6},{6,7},{7,8},{8,9},{9,10},{10,1... | collective-permute-start | bytes 6152 | tf_op jit(solution)/shard_map/ppermute | solution.py:110
  33.6 3.1 %collective-permute-start.14 = (bf16[32,32]{1,0:T(8,128)(2,1)S(1)}, bf16[32,32]{1,0:T(8,128)(2,1)S(1)}, u32[]{:S(2)}, u32[]{:S(2)}) collective-permute-start(bf16[32,32]{1,0:T(8,128)(2,1)S(1)} %copy-done.4), channel_id=1, source_target_pairs={{0,15},{1,0},{2,1},{3,2},{4,3},{5,4},{6,5},{7,6},{8,7},{9,8},{10,9... | collective-permute-start | bytes 6152 | tf_op jit(solution)/shard_map/ppermute | solution.py:110
  37.9 9.8 %copy-start.1 = (bf16[32,1024]{1,0:T(8,128)(2,1)S(1)}, bf16[32,1024]{1,0:T(8,128)(2,1)}, u32[]{:S(2)}) copy-start(bf16[32,1024]{1,0:T(8,128)(2,1)} %up_ref.1) | copy-start | bytes 196612
  37.9 5.0 %collective-permute-start.16 = (f32[32,32]{1,0:T(8,128)S(1)}, f32[32,32]{1,0:T(8,128)S(1)}, u32[]{:S(2)}, u32[]{:S(2)}) collective-permute-start(f32[32,32]{1,0:T(8,128)S(1)} %get-tuple-element.21), channel_id=1, source_target_pairs={{0,1},{1,3},{2,5},{3,7},{4,9},{5,11},{6,13},{7,15},{8,17},{9,19},{... | collective-permute-start | bytes 12296 | tf_op jit(solution)/shard_map/ppermute | solution.py:145
  39.8 7.8 %collective-permute-start.15 = (f32[32,32]{1,0:T(8,128)S(1)}, f32[32,32]{1,0:T(8,128)S(1)}, u32[]{:S(2)}, u32[]{:S(2)}) collective-permute-start(f32[32,32]{1,0:T(8,128)S(1)} %get-tuple-element.22), channel_id=1, source_target_pairs={{0,0},{1,2},{2,4},{3,6},{4,8},{5,10},{6,12},{7,14},{8,16},{9,18},{... | collective-permute-start | bytes 12296 | tf_op jit(solution)/shard_map/ppermute | solution.py:145

commit v2 on v1

v2 whole, which is shorter than its diff:
```python
import functools

import jax
import jax.numpy as jnp
from jax import lax
from jax.experimental import pallas as pl
from jax.experimental.pallas import tpu as pltpu
from jax.sharding import PartitionSpec as P

HS = 64
LANES = 128
CUT = 16

adapter_factor = 2.0

NT = (((1,), (1,)), ((), ()))
TN = (((0,), (0,)), ((), ()))


def dot(left, right, dims):
    return lax.dot_general(left, right, dims, preferred_element_type=jnp.float32)


def source_range(source_ref, target_ref, count):
    position = lax.broadcasted_iota(jnp.int32, (1, count), 1)
    first = jnp.zeros((1, count), jnp.int32)
    last = jnp.zeros((1, count), jnp.int32)
    target_start = jnp.int32(0)
    source_start = jnp.int32(0)
    for i in range(source_ref.shape[1]):
        source_end = source_start + source_ref[0, i]
        inside = position >= target_start
        first = jnp.where(inside, source_start, first)
        last = jnp.where(inside, source_end, last)
        target_start = target_start + target_ref[0, i]
        source_start = source_end
    return first, last


def attention_kernel(dp, mp, source_any, target_any, query_ref, grad_ref, kv_ref, *refs):
    low_refs = refs[:dp]
    query_grad_ref, both_grad_ref = refs[dp:dp + 2]
    piece_refs = refs[dp + 2:dp + 2 + dp]
    source_ref, target_ref, pieces, sems = refs[dp + 2 + dp:]
    source_copy = pltpu.make_async_copy(source_any, source_ref, sems.at[0])
    target_copy = pltpu.make_async_copy(target_any, target_ref, sems.at[1])
    source_copy.start()
    target_copy.start()
    tgt_count = query_ref.shape[1]
    src_count = kv_ref.shape[0]
    rows = src_count // mp
    both = kv_ref[...]
    query_t = query_ref[...]
    grad_t = grad_ref[...]
    blank = jnp.zeros_like(query_t)
    query_wide = jnp.concatenate([query_t, blank], axis=0)
    grad_wide = jnp.concatenate([blank, grad_t], axis=0)
    scores = jnp.dot(both, query_wide, preferred_element_type=jnp.float32)
    dprob = jnp.dot(both, grad_wide, preferred_element_type=jnp.float32)
    source_copy.wait()
    target_copy.wait()
    first, last = source_range(source_ref, target_ref, tgt_count)
    position = lax.broadcasted_iota(jnp.int32, scores.shape, 0)
    allowed = jnp.logical_and(position >= first, position < last)
    expo = jnp.where(allowed, jnp.exp(scores), 0.0)
    total = jnp.sum(expo, axis=0, keepdims=True)
    delta = jnp.sum(expo * dprob, axis=0, keepdims=True) / total
    prob = expo * (1.0 / total)
    prob_low = prob.astype(jnp.bfloat16)
    dscore = (prob * (dprob - delta)).astype(jnp.bfloat16)
    both_grad = dot(dscore, query_wide, NT) + dot(prob_low, grad_wide, NT)
    both_low = both_grad.astype(jnp.bfloat16)

    both_rank = low_refs[0].shape[1]
    mine = lax.axis_index("dp")
    parts = []
    for low_ref in low_refs:
        for cut in range(rows // CUT):
            parts.append(low_ref[cut * CUT:(cut + 1) * CUT, :])
    side = LANES // both_rank
    packed = [
        jnp.concatenate(parts[at:at + side], axis=1) for at in range(0, len(parts), side)
    ]
    packed = jnp.concatenate(packed, axis=0) if len(packed) > 1 else packed[0]
    for block in range(mp):
        both_grad_ref[block, :rows, :] = both_low[block * rows:(block + 1) * rows]
        both_grad_ref[block, rows:, :] = packed

    order = []
    for cut in range(rows // CUT):
        for block in range(mp):
            start = block * rows + cut * CUT
            order.append(both_low[start:start + CUT])
    turned = jnp.concatenate(order, axis=0).astype(jnp.float32).T.astype(jnp.bfloat16)
    step = HS // dp
    for j in range(dp):
        pieces[j] = jnp.concatenate(
            [turned[j * step:(j + 1) * step], turned[HS + j * step:HS + (j + 1) * step]], axis=0
        )
    for s in range(dp):
        piece_refs[s][...] = pieces[lax.rem(mine + s, dp)]

    query_grad = dot(both, dscore, TN)
    query_grad_ref[...] = query_grad[:HS].astype(jnp.bfloat16)


def owner_kernel(dp, mp, got_ref, up_ref, *refs):
    piece_refs = refs[:dp]
    key_ref, value_ref, low_grad_ref, up_grad_ref = refs[dp:dp + 4]
    rows = key_ref.shape[0]
    both_rank = up_ref.shape[0]
    rank = both_rank // 2
    for pair in range(mp // 2):
        first = got_ref[2 * pair, :rows, :]
        second = got_ref[2 * pair + 1, :rows, :]
        columns = slice(2 * pair * HS, (2 * pair + 2) * HS)
        key_ref[:, columns] = jnp.concatenate([first[:, :HS], second[:, :HS]], axis=1)
        value_ref[:, columns] = jnp.concatenate([first[:, HS:], second[:, HS:]], axis=1)
    up = up_ref[...]
    from_key = dot(key_ref[...], up, NT)
    from_value = dot(value_ref[...], up, NT)
    column = lax.broadcasted_iota(jnp.int32, from_key.shape, 1)
    low_grad_ref[...] = adapter_factor * jnp.where(column < rank, from_key, from_value)

    me = lax.axis_index("dp") * mp + lax.axis_index("mp")
    side = LANES // both_rank
    cuts = rows // CUT
    half = mp * CUT
    step = HS // dp
    lane = lax.broadcasted_iota(jnp.int32, (2 * step, LANES), 1) // both_rank
    total = jnp.zeros((2 * step, LANES), jnp.float32)
    lows = []
    for group in range(dp * cuts // side):
        at = rows + group * CUT
        lows.append(jnp.concatenate([got_ref[block, at:at + CUT, :] for block in range(mp)], axis=0))
    for s in range(dp):
        pack = lax.rem(lax.rem(me, dp) + dp - s, dp)
        for cut in range(cuts):
            piece = piece_refs[s][:, cut * half:(cut + 1) * half]
            slot = pack * cuts + cut
            for group, low in enumerate(lows):
                product = jnp.dot(piece, low, preferred_element_type=jnp.float32)
                total += jnp.where(lane + group * side == slot, product, 0.0)
    share = total[:, :both_rank]
    for at in range(1, side):
        share += total[:, at * both_rank:(at + 1) * both_rank]
    column = lax.broadcasted_iota(jnp.int32, (step, both_rank), 1)
    up_grad_ref[...] = adapter_factor * jnp.where(column < rank, share[:step], share[step:])


def local(dp, mp, query, kv_cache, out_grad, source_lengths, target_lengths, low_rank, adapter_up_matrix):
    tgt_count = query.shape[0]
    src_count = kv_cache.shape[0]
    rows, both_rank = low_rank.shape
    width = adapter_up_matrix.shape[1]
    step = HS // dp
    low_rows = dp * rows * both_rank // LANES
    vmem = pl.BlockSpec(memory_space=pltpu.VMEM)
    hbm = pl.BlockSpec(memory_space=pl.ANY)
    params = pltpu.CompilerParams(vmem_limit_bytes=48 * 1024 * 1024)

    seen = [low_rank]
    for s in range(1, dp):
        seen.append(lax.ppermute(low_rank, "dp", [(d, (d + s) % dp) for d in range(dp)]))
    mine = lax.axis_index("dp")
    lows = []
    for pack in range(dp):
        low = seen[0]
        for s in range(1, dp):
            low = jnp.where((mine - s) % dp == pack, seen[s], low)
        lows.append(low)

    query_grad_t, sent, *pieces = pl.pallas_call(
        functools.partial(attention_kernel, dp, mp),
        out_shape=[
            jax.ShapeDtypeStruct((HS, tgt_count), jnp.bfloat16),
            jax.ShapeDtypeStruct((mp, rows + low_rows, LANES), jnp.bfloat16),
        ] + [jax.ShapeDtypeStruct((2 * step, src_count), jnp.bfloat16)] * dp,
        in_specs=[hbm, hbm] + [vmem] * (3 + dp),
        out_specs=[vmem] * (2 + dp),
        scratch_shapes=[
            pltpu.SMEM(source_lengths.shape, jnp.int32),
            pltpu.SMEM(target_lengths.shape, jnp.int32),
            pltpu.VMEM((dp, 2 * step, src_count), jnp.bfloat16),
            pltpu.SemaphoreType.DMA((2,)),
        ],
        compiler_params=params,
        name="attention_backward",
    )(source_lengths, target_lengths, query.T, out_grad.T, kv_cache, *lows)

    got = lax.all_to_all(sent, "mp", split_axis=0, concat_axis=0, tiled=True)

    arrived = []
    for s in range(dp):
        route = [(d * mp + h, h * dp + (d + s) % dp) for d in range(dp) for h in range(mp)]
        arrived.append(lax.ppermute(pieces[s], ("dp", "mp"), route))

    key_gradient, value_grad, low_grad, up_grad = pl.pallas_call(
        functools.partial(owner_kernel, dp, mp),
        out_shape=[
            jax.ShapeDtypeStruct((rows, width), jnp.bfloat16),
            jax.ShapeDtypeStruct((rows, width), jnp.bfloat16),
            jax.ShapeDtypeStruct((rows, both_rank), jnp.float32),
            jax.ShapeDtypeStruct((step, both_rank), jnp.float32),
        ],
        in_specs=[vmem] * (2 + dp),
        out_specs=[vmem] * 4,
        compiler_params=params,
        name="owner_outputs",
    )(got, adapter_up_matrix, *arrived)
    return query_grad_t.T, key_gradient, value_grad, low_grad, up_grad


def solution(mesh):
    in_specs = (
        P("dp", "mp"),
        P("dp", "mp"),
        P("dp", "mp"),
        P("dp", None),
        P("dp", None),
        P(("dp", "mp"), None),
        P(),
    )
    out_specs = (
        P("dp", "mp"),
        P(("dp", "mp"), None),
        P(("dp", "mp"), None),
        P(("dp", "mp"), None),
        P(("dp", "mp"), None),
    )
    body = functools.partial(local, mesh.shape["dp"], mesh.shape["mp"])
    return jax.shard_map(body, mesh=mesh, in_specs=in_specs, out_specs=out_specs, check_vma=False)
```

time: 48.9 us -> 26.5 us (0.54)
  the two profiles are of different devices: /device:TPU:25 before, /device:TPU:4 now
where the time goes in v2:
time: 26.5 us; the launch traced here: 26.3 us
  waiting for transfers between devices  12.4 us (47%)
  starting transfers between devices  8.61 us (32%)
  Pallas kernels  2.97 us (11%)
  local copies, waits for them, and re-layouts  1.56 us (6%)
  between operations  0.76 us (3%)
    ppermute x2, waiting for transfers between devices, local(): arrived.append(lax.ppermute(pieces[s], ('dp', 'mp'), route))  8.55 us
    all_to_all x1, starting transfers between devices, local(): got = lax.all_to_all(sent, 'mp', split_axis=0, concat_axis=0, tiled=True)  6.05 us
    ppermute x1, waiting for transfers between devices, local(): lax.ppermute(low_rank, 'dp', [(d, (d + s) % dp) for d in range(dp)])  3.8 us
    ppermute x2, starting transfers between devices, local(): arrived.append(lax.ppermute(pieces[s], ('dp', 'mp'), route))  2.48 us
    pallas_call x1, Pallas kernels, local(): pl.pallas_call(functools.partial(attention_kernel, dp, mp), out_shape=[ja...  1.98 us
    unnamed x14, local copies, waits for them, and re-layouts  1.56 us
    pallas_call x1, Pallas kernels, local(): pl.pallas_call(functools.partial(owner_kernel, dp, mp), out_shape=[jax.Sh...  0.99 us
  transfers between devices with their start and end apart: 4, of which 3 were waited for; matrix products, arithmetic and copies ran while one was open for 0% of the time, Pallas kernels for 0%

profile of v2, /device:TPU:4, one launch (start us, length us, event | category | flops | bytes accessed | tf_op | source)
XLA Modules:
  0.0 26.3 jit_solution(7772451578216142373)
XLA Ops:
  0.6 0.1 collective-permute-start
  0.7 0.0 copy-start.6
  0.7 0.0 copy-start.3
  0.7 0.0 copy-start.2
  0.8 3.8 %collective-permute-done = bf16[32,32]{1,0:T(8,128)(2,1)S(1)} collective-permute-done((bf16[32,32]{1,0:T(8,128)(2,1)}, bf16[32,32]{1,0:T(8,128)(2,1)S(1)}, u32[]{:S(2)}, u32[]{:S(2)}) %collective-permute-start) | collective-permute-done | bytes 2080 | tf_op jit(solution)/shard_map/ppermute | solution.py:164
  4.6 0.0 copy-done.6
  4.6 0.0 copy-start.4
  4.6 0.0 copy-start.5
  4.6 0.0 copy-done.3
  4.6 0.0 copy-done.2
  4.6 0.6 %copy-done.4 = s32[1,8]{1,0:T(1,128)S(1)} copy-done((s32[1,8]{1,0:T(1,128)S(1)}, s32[1,8]{1,0:T(1,128)}, u32[]{:S(2)}) %copy-start.4) | copy-done | bytes 56
  5.2 0.0 copy-done.5
  5.2 0.0 copy-start
  5.2 0.9 %copy-done = bf16[512,128]{1,0:T(8,128)(2,1)S(1)} copy-done((bf16[512,128]{1,0:T(8,128)(2,1)S(1)}, bf16[512,128]{1,0:T(8,128)(2,1)}, u32[]{:S(2)}) %copy-start) | copy-done | bytes 131096
  6.1 2.0 %attention_backward.1 = (bf16[64,256]{1,0:T(8,128)(2,1)}, bf16[16,48,128]{2,1,0:T(8,128)(2,1)}, bf16[64,512]{1,0:T(8,128)(2,1)S(1)}, bf16[64,512]{1,0:T(8,128)(2,1)S(1)}) custom-call(s32[1,8]{1,0:T(1,128)S(1)} %copy-done.4, s32[1,8]{1,0:T(1,128)S(1)} %copy-done.5, bf16[64,256]{1,0:T(8,128)(2,1)S(1)} %bitcast.3, bf16[64,256]{1,0:T(8,128)(2,1)S(1)} %bitcast.4, ...), custom_call_target="tpu_custom_call" | custom-call | tf_op jit(solution)/shard_map/attention_backward/pallas_call | solution.py:173
  8.1 0.0 copy-start.1
  8.1 6.1 %all-to-all-start = ((bf16[16,48,128]{2,1,0:T(8,128)(2,1)}), bf16[16,48,128]{2,1,0:T(8,128)(2,1)S(1)}, u32[]{:S(2)}, u32[]{:S(2)}) async-start(bf16[16,48,128]{2,1,0:T(8,128)(2,1)} %get-tuple-element.14), calls=%async_computation | async-start | bytes 393216 | tf_op jit(solution)/shard_map/all_to_all | solution.py:191
  14.2 2.4 %collective-permute-start.1 = (bf16[64,512]{1,0:T(8,128)(2,1)S(1)}, bf16[64,512]{1,0:T(8,128)(2,1)S(1)}, u32[]{:S(2)}, u32[]{:S(2)}) collective-permute-start(bf16[64,512]{1,0:T(8,128)(2,1)S(1)} %get-tuple-element.15), channel_id=1, source_target_pairs={{0,0},{1,2},{2,4},{3,6},{4,8},{5,10},{6,12},{7,14},{8,16},{9,18},{... | collective-permute-start | bytes 196616 | tf_op jit(solution)/shard_map/ppermute | solution.py:196
  16.6 0.1 collective-permute-start.2
  16.7 7.2 %collective-permute-done.1.refs_0_ = bf16[64,512]{1,0:T(8,128)(2,1)S(1)} collective-permute-done((bf16[64,512]{1,0:T(8,128)(2,1)S(1)}, bf16[64,512]{1,0:T(8,128)(2,1)S(1)}, u32[]{:S(2)}, u32[]{:S(2)}) %collective-permute-start.1) | collective-permute-done | bytes 65568 | tf_op jit(solution)/shard_map/ppermute | solution.py:196
  23.9 1.4 %collective-permute-done.2.refs_1_ = bf16[64,512]{1,0:T(8,128)(2,1)S(1)} collective-permute-done((bf16[64,512]{1,0:T(8,128)(2,1)S(1)}, bf16[64,512]{1,0:T(8,128)(2,1)S(1)}, u32[]{:S(2)}, u32[]{:S(2)}) %collective-permute-start.2) | collective-permute-done | bytes 65568 | tf_op jit(solution)/shard_map/ppermute | solution.py:196
  25.3 0.0 all-to-all-done.got_ref
  25.3 0.0 copy-done.1
  25.3 1.0 %owner_outputs.1 = (bf16[32,1024]{1,0:T(8,128)(2,1)}, bf16[32,1024]{1,0:T(8,128)(2,1)}, f32[32,32]{1,0:T(8,128)}, f32[32,32]{1,0:T(8,128)}) custom-call(bf16[16,48,128]{2,1,0:T(8,128)(2,1)S(1)} %all-to-all-done.got_ref, bf16[32,1024]{1,0:T(8,128)(2,1)S(1)} %copy-done.1, bf16[64,512]{1,0:T(8,128)(2,1)S(1)} %collective-permute-done.1.refs_0_, ...), custom_call_target="tpu_custom_call" | custom-call | tf_op jit(solution)/shard_map/owner_outputs/pallas_call | solution.py:198
  (1 shorter events, 0.0 us)
Async XLA Ops:
  0.6 3.9 %collective-permute-start = (bf16[32,32]{1,0:T(8,128)(2,1)}, bf16[32,32]{1,0:T(8,128)(2,1)S(1)}, u32[]{:S(2)}, u32[]{:S(2)}) collective-permute-start(bf16[32,32]{1,0:T(8,128)(2,1)} %param.12), channel_id=1, source_target_pairs={{0,16},{16,0},{1,17},{17,1},{2,18},{18,2},{3,19},{19,3},{4,20},{20... | collective-permute-start | bytes 6152 | tf_op jit(solution)/shard_map/ppermute | solution.py:164
  0.7 3.9 %copy-start.6 = (bf16[32,32]{1,0:T(8,128)(2,1)S(1)}, bf16[32,32]{1,0:T(8,128)(2,1)}, u32[]{:S(2)}) copy-start(bf16[32,32]{1,0:T(8,128)(2,1)} %param.12) | copy-start | bytes 6148
  0.7 3.9 %copy-start.3 = (bf16[256,64]{0,1:T(8,128)(2,1)S(1)}, bf16[256,64]{0,1:T(8,128)(2,1)}, u32[]{:S(2)}) copy-start(bf16[256,64]{0,1:T(8,128)(2,1)} %param.9) | copy-start | bytes 98308
  0.7 3.9 %copy-start.2 = (bf16[256,64]{0,1:T(8,128)(2,1)S(1)}, bf16[256,64]{0,1:T(8,128)(2,1)}, u32[]{:S(2)}) copy-start(bf16[256,64]{0,1:T(8,128)(2,1)} %param.7) | copy-start | bytes 98308
  4.6 0.7 %copy-start.4 = (s32[1,8]{1,0:T(1,128)S(1)}, s32[1,8]{1,0:T(1,128)}, u32[]{:S(2)}) copy-start(s32[1,8]{1,0:T(1,128)} %source_any.1) | copy-start | bytes 100
  4.6 0.7 %copy-start.5 = (s32[1,8]{1,0:T(1,128)S(1)}, s32[1,8]{1,0:T(1,128)}, u32[]{:S(2)}) copy-start(s32[1,8]{1,0:T(1,128)} %target_any.1) | copy-start | bytes 100
  5.2 0.9 %copy-start = (bf16[512,128]{1,0:T(8,128)(2,1)S(1)}, bf16[512,128]{1,0:T(8,128)(2,1)}, u32[]{:S(2)}) copy-start(bf16[512,128]{1,0:T(8,128)(2,1)} %kv_ref.1) | copy-start | bytes 393220
  8.1 17.1 %copy-start.1 = (bf16[32,1024]{1,0:T(8,128)(2,1)S(1)}, bf16[32,1024]{1,0:T(8,128)(2,1)}, u32[]{:S(2)}) copy-start(bf16[32,1024]{1,0:T(8,128)(2,1)} %up_ref.1) | copy-start | bytes 196612
  8.1 17.1 %all-to-all-start = ((bf16[16,48,128]{2,1,0:T(8,128)(2,1)}), bf16[16,48,128]{2,1,0:T(8,128)(2,1)S(1)}, u32[]{:S(2)}, u32[]{:S(2)}) async-start(bf16[16,48,128]{2,1,0:T(8,128)(2,1)} %get-tuple-element.14), calls=%async_computation | async-start | bytes 393216 | tf_op jit(solution)/shard_map/all_to_all | solution.py:191
  14.2 9.7 %collective-permute-start.1 = (bf16[64,512]{1,0:T(8,128)(2,1)S(1)}, bf16[64,512]{1,0:T(8,128)(2,1)S(1)}, u32[]{:S(2)}, u32[]{:S(2)}) collective-permute-start(bf16[64,512]{1,0:T(8,128)(2,1)S(1)} %get-tuple-element.15), channel_id=1, source_target_pairs={{0,0},{1,2},{2,4},{3,6},{4,8},{5,10},{6,12},{7,14},{8,16},{9,18},{... | collective-permute-start | bytes 196616 | tf_op jit(solution)/shard_map/ppermute | solution.py:196
  16.6 8.6 %collective-permute-start.2 = (bf16[64,512]{1,0:T(8,128)(2,1)S(1)}, bf16[64,512]{1,0:T(8,128)(2,1)S(1)}, u32[]{:S(2)}, u32[]{:S(2)}) collective-permute-start(bf16[64,512]{1,0:T(8,128)(2,1)S(1)} %get-tuple-element.16), channel_id=1, source_target_pairs={{0,1},{1,3},{2,5},{3,7},{4,9},{5,11},{6,13},{7,15},{8,17},{9,19},{... | collective-permute-start | bytes 196616 | tf_op jit(solution)/shard_map/ppermute | solution.py:196

commit v3 on v2

v3 whole, which is shorter than its diff:
```python
import functools

import jax
import jax.numpy as jnp
from jax import lax
from jax.experimental import pallas as pl
from jax.experimental.pallas import tpu as pltpu
from jax.sharding import PartitionSpec as P

HS = 64
LANES = 128
CUT = 16

adapter_factor = 2.0

NT = (((1,), (1,)), ((), ()))
TN = (((0,), (0,)), ((), ()))


def dot(left, right, dims):
    return lax.dot_general(left, right, dims, preferred_element_type=jnp.float32)


def source_range(source_ref, target_ref, count):
    position = lax.broadcasted_iota(jnp.int32, (1, count), 1)
    first = jnp.zeros((1, count), jnp.int32)
    last = jnp.zeros((1, count), jnp.int32)
    target_start = jnp.int32(0)
    source_start = jnp.int32(0)
    for i in range(source_ref.shape[1]):
        source_end = source_start + source_ref[0, i]
        inside = position >= target_start
        first = jnp.where(inside, source_start, first)
        last = jnp.where(inside, source_end, last)
        target_start = target_start + target_ref[0, i]
        source_start = source_end
    return first, last


def attention_kernel(
    inner, outer,
    source_any, target_any, query_any, grad_any, kv_any, low_any,
    query_grad_ref, sent_ref,
    source_ref, target_ref, query_ref, grad_ref, kv_ref, low_ref, sems,
):
    pairs = [
        (kv_any, kv_ref), (query_any, query_ref), (grad_any, grad_ref),
        (source_any, source_ref), (target_any, target_ref), (low_any, low_ref),
    ]
    copies = [
        pltpu.make_async_copy(here, there, sems.at[i]) for i, (here, there) in enumerate(pairs)
    ]
    for copy in copies:
        copy.start()
    for copy in copies:
        copy.wait()
    tgt_count = query_ref.shape[1]
    rows = kv_ref.shape[0] // (inner * outer)
    both = kv_ref[...]
    query_t = query_ref[...]
    grad_t = grad_ref[...]
    blank = jnp.zeros_like(query_t)
    query_wide = jnp.concatenate([query_t, blank], axis=0)
    grad_wide = jnp.concatenate([blank, grad_t], axis=0)
    scores = jnp.dot(both, query_wide, preferred_element_type=jnp.float32)
    dprob = jnp.dot(both, grad_wide, preferred_element_type=jnp.float32)
    first, last = source_range(source_ref, target_ref, tgt_count)
    position = lax.broadcasted_iota(jnp.int32, scores.shape, 0)
    allowed = jnp.logical_and(position >= first, position < last)
    expo = jnp.where(allowed, jnp.exp(scores), 0.0)
    total = jnp.sum(expo, axis=0, keepdims=True)
    delta = jnp.sum(expo * dprob, axis=0, keepdims=True) / total
    prob = expo * (1.0 / total)
    prob_low = prob.astype(jnp.bfloat16)
    dscore = (prob * (dprob - delta)).astype(jnp.bfloat16)
    both_grad = dot(dscore, query_wide, NT) + dot(prob_low, grad_wide, NT)
    both_low = both_grad.astype(jnp.bfloat16)
    low = low_ref[...]
    cuts = rows // CUT
    spread = [low[cut * CUT:(cut + 1) * CUT] for cut in range(cuts)]
    spread.append(jnp.zeros((CUT, LANES - cuts * low.shape[1]), jnp.bfloat16))
    spread = jnp.concatenate(spread, axis=1)
    for p in range(inner):
        for z in range(outer):
            block = z * inner + p
            sent_ref[p, z * rows:(z + 1) * rows, :] = both_low[block * rows:(block + 1) * rows]
        sent_ref[p, outer * rows:, :] = spread
    query_grad = dot(both, dscore, TN)
    query_grad_ref[...] = query_grad[:HS].astype(jnp.bfloat16)


def relay_kernel(inner, outer, both_rank, got_ref, *out_refs):
    here = lax.axis_index("mp") // inner
    rows = (got_ref.shape[1] - CUT) // outer
    used = rows // CUT * both_rank
    beside = LANES // used
    groups = []
    for g in range(0, inner, beside):
        parts = [got_ref[g + q, outer * rows:, :][:, :used] for q in range(beside)]
        groups.append(jnp.concatenate(parts, axis=1))
    for l, out_ref in enumerate(out_refs):
        there = here ^ l
        for p in range(inner):
            out_ref[p * rows:(p + 1) * rows, :] = got_ref[
                p, pl.ds(pl.multiple_of(there * rows, rows), rows), :
            ]
        for g, group in enumerate(groups):
            at = inner * rows + g * CUT
            out_ref[at:at + CUT, :] = group


def share_kernel(inner, outer, both_rank, rows, sent_ref, *refs):
    plane_refs = refs[:outer]
    out_refs = refs[outer:]
    here = lax.axis_index("mp") // inner
    mine = lax.axis_index("dp")
    dp = len(out_refs)
    cuts = rows // CUT
    beside = LANES // (cuts * both_rank)
    lows = jnp.concatenate([ref[inner * rows:, :] for ref in plane_refs], axis=0)
    lane = lax.broadcasted_iota(jnp.int32, (2 * HS, LANES), 1) // both_rank
    total = jnp.zeros((2 * HS, LANES), jnp.float32)
    for q in range(beside):
        for cut in range(cuts):
            tokens = []
            for l in range(outer):
                start = (here ^ l) * rows + cut * CUT
                for g in range(inner // beside):
                    tokens.append(sent_ref[g * beside + q, pl.ds(pl.multiple_of(start, CUT), CUT), :])
            product = dot(jnp.concatenate(tokens, axis=0), lows, TN)
            total += jnp.where(lane == q * cuts + cut, product, 0.0)
    share = total[:, :both_rank]
    for at in range(1, beside * cuts):
        share += total[:, at * both_rank:(at + 1) * both_rank]
    column = lax.broadcasted_iota(jnp.int32, (HS, both_rank), 1)
    share = adapter_factor * jnp.where(column < both_rank // 2, share[:HS], share[HS:])
    step = HS // dp
    for s, out_ref in enumerate(out_refs):
        turn = lax.rem(mine + s, dp)
        piece = share[:step]
        for j in range(1, dp):
            piece = jnp.where(turn == j, share[j * step:(j + 1) * step], piece)
        out_ref[...] = piece


def owner_kernel(inner, outer, up_ref, *refs):
    plane_refs = refs[:outer]
    key_ref, value_ref, low_grad_ref = refs[outer:]
    here = lax.axis_index("mp") // inner
    rows = key_ref.shape[0]
    rank = up_ref.shape[0] // 2
    for l, plane_ref in enumerate(plane_refs):
        columns = pl.ds(pl.multiple_of((here ^ l) * (inner * HS), LANES), inner * HS)
        keys = []
        values = []
        for p in range(inner):
            block = plane_ref[p * rows:(p + 1) * rows, :]
            keys.append(block[:, :HS])
            values.append(block[:, HS:])
        key_ref[:, columns] = jnp.concatenate(keys, axis=1)
        value_ref[:, columns] = jnp.concatenate(values, axis=1)
    up = up_ref[...]
    from_key = dot(key_ref[...], up, NT)
    from_value = dot(value_ref[...], up, NT)
    column = lax.broadcasted_iota(jnp.int32, from_key.shape, 1)
    low_grad_ref[...] = adapter_factor * jnp.where(column < rank, from_key, from_value)


def local(dp, mp, query, kv_cache, out_grad, source_lengths, target_lengths, low_rank, adapter_up_matrix):
    tgt_count = query.shape[0]
    src_count = kv_cache.shape[0]
    rows, both_rank = low_rank.shape
    width = adapter_up_matrix.shape[1]
    step = HS // dp
    inner = 1
    while inner * inner * 4 <= mp:
        inner *= 2
    inner = min(2 * inner, mp) if inner * inner < mp else inner
    outer = mp // inner
    assert outer & (outer - 1) == 0
    vmem = pl.BlockSpec(memory_space=pltpu.VMEM)
    hbm = pl.BlockSpec(memory_space=pl.ANY)
    params = pltpu.CompilerParams(vmem_limit_bytes=48 * 1024 * 1024)
    whole_vmem = pltpu.CompilerParams(vmem_limit_bytes=60 * 1024 * 1024)

    query_t = query.T
    grad_t = out_grad.T
    query_grad_t, sent = pl.pallas_call(
        functools.partial(attention_kernel, inner, outer),
        out_shape=[
            jax.ShapeDtypeStruct((HS, tgt_count), jnp.bfloat16),
            jax.ShapeDtypeStruct((inner, outer * rows + CUT, LANES), jnp.bfloat16),
        ],
        in_specs=[hbm] * 6,
        out_specs=[vmem] * 2,
        scratch_shapes=[
            pltpu.SMEM(source_lengths.shape, jnp.int32),
            pltpu.SMEM(target_lengths.shape, jnp.int32),
            pltpu.VMEM(query_t.shape, jnp.bfloat16),
            pltpu.VMEM(grad_t.shape, jnp.bfloat16),
            pltpu.VMEM(kv_cache.shape, jnp.bfloat16),
            pltpu.VMEM(low_rank.shape, jnp.bfloat16),
            pltpu.SemaphoreType.DMA((6,)),
        ],
        compiler_params=whole_vmem,
        name="attention_backward",
    )(source_lengths, target_lengths, query_t, grad_t, kv_cache, low_rank)

    planes = [[z * inner + p for p in range(inner)] for z in range(outer)]
    got = lax.all_to_all(sent, "mp", 0, 0, axis_index_groups=planes, tiled=True)

    plane_rows = inner * rows + inner * rows * both_rank // LANES
    relayed = pl.pallas_call(
        functools.partial(relay_kernel, inner, outer, both_rank),
        out_shape=[jax.ShapeDtypeStruct((plane_rows, LANES), jnp.bfloat16)] * outer,
        in_specs=[vmem],
        out_specs=[vmem] * outer,
        compiler_params=params,
        name="relay",
    )(got)
    arrived = [relayed[0]]
    for l in range(1, outer):
        route = [(m, ((m // inner) ^ l) * inner + m % inner) for m in range(mp)]
        arrived.append(lax.ppermute(relayed[l], "mp", route))

    shares = pl.pallas_call(
        functools.partial(share_kernel, inner, outer, both_rank, rows),
        out_shape=[jax.ShapeDtypeStruct((step, both_rank), jnp.float32)] * dp,
        in_specs=[vmem] * (1 + outer),
        out_specs=[vmem] * dp,
        compiler_params=params,
        name="adapter_shares",
    )(sent, *arrived)

    up_grad = None
    for s in range(dp):
        route = [(d * mp + h, h * dp + (d + s) % dp) for d in range(dp) for h in range(mp)]
        term = lax.ppermute(shares[s], ("dp", "mp"), route)
        up_grad = term if up_grad is None else up_grad + term

    key_gradient, value_grad, low_grad = pl.pallas_call(
        functools.partial(owner_kernel, inner, outer),
        out_shape=[
            jax.ShapeDtypeStruct((rows, width), jnp.bfloat16),
            jax.ShapeDtypeStruct((rows, width), jnp.bfloat16),
            jax.ShapeDtypeStruct((rows, both_rank), jnp.float32),
        ],
        in_specs=[vmem] * (1 + outer),
        out_specs=[vmem] * 3,
        compiler_params=params,
        name="owner_outputs",
    )(adapter_up_matrix, *arrived)
    return query_grad_t.T, key_gradient, value_grad, low_grad, up_grad


def solution(mesh):
    in_specs = (
        P("dp", "mp"),
        P("dp", "mp"),
        P("dp", "mp"),
        P("dp", None),
        P("dp", None),
        P(("dp", "mp"), None),
        P(),
    )
    out_specs = (
        P("dp", "mp"),
        P(("dp", "mp"), None),
        P(("dp", "mp"), None),
        P(("dp", "mp"), None),
        P(("dp", "mp"), None),
    )
    body = functools.partial(local, mesh.shape["dp"], mesh.shape["mp"])
    return jax.shard_map(body, mesh=mesh, in_specs=in_specs, out_specs=out_specs, check_vma=False)
```

time: 26.5 us -> 30.4 us (1.15)
  the two profiles are of different devices: /device:TPU:4 before, /device:TPU:16 now
where the time goes in v3:
time: 30.4 us; the launch traced here: 30.1 us
  starting transfers between devices  9.28 us (31%)
  blocking collectives  8.12 us (27%)
  waiting for transfers between devices  7.69 us (25%)
  Pallas kernels  3.7 us (12%)
  between operations  0.68 us (2%)
  other arithmetic  0.61 us (2%)
    all_to_all x1, blocking collectives, local(): got = lax.all_to_all(sent, 'mp', 0, 0, axis_index_groups=planes, tiled=True)  8.12 us
    ppermute x2, starting transfers between devices, local(): term = lax.ppermute(shares[s], ('dp', 'mp'), route)  5.78 us
    ppermute x3, waiting for transfers between devices, local(): arrived.append(lax.ppermute(relayed[l], 'mp', route))  3.96 us
    ppermute x2, waiting for transfers between devices, local(): term = lax.ppermute(shares[s], ('dp', 'mp'), route)  3.73 us
    ppermute x3, starting transfers between devices, local(): arrived.append(lax.ppermute(relayed[l], 'mp', route))  3.5 us
    pallas_call x1, Pallas kernels, local(): pl.pallas_call(functools.partial(attention_kernel, inner, outer), out_sha...  2.41 us
    pallas_call x1, Pallas kernels, local(): pl.pallas_call(functools.partial(owner_kernel, inner, outer), out_shape=[...  0.88 us
    add x1, other arithmetic, local(): up_grad = term if up_grad is None else up_grad + term  0.61 us
  transfers between devices with their start and end apart: 5, of which 5 were waited for; matrix products, arithmetic and copies ran while one was open for 0% of the time, Pallas kernels for 3%

profile of v3, /device:TPU:16, one launch (start us, length us, event | category | flops | bytes accessed | tf_op | source)
XLA Modules:
  0.0 30.1 jit_solution(4671242918973861508)
XLA Ops:
  0.6 2.4 %attention_backward.1 = (bf16[64,256]{1,0:T(8,128)(2,1)}, bf16[4,144,128]{2,1,0:T(8,128)(2,1)}) custom-call(s32[1,8]{1,0:T(1,128)} %source_any.1, s32[1,8]{1,0:T(1,128)} %target_any.1, bf16[64,256]{1,0:T(8,128)(2,1)} %bitcast.3, bf16[64,256]{1,0:T(8,128)(2,1)} %bitcast.4, bf16[512,128]{1,0:T(8,128)(2,1)} %kv_any.1, bf16[32,32]{1,0:T(8,128)(2,1)} %low_any.1), custom_call_target="tpu_custom_call" | custom-call | tf_op jit(solution)/shard_map/attention_backward/pallas_call | solution.py:188
  3.0 8.1 %all_to_all.5.got_ref = bf16[4,144,128]{2,1,0:T(8,128)(2,1)S(1)} all-to-all(bf16[4,144,128]{2,1,0:T(8,128)(2,1)} %get-tuple-element.17.sent_ref), channel_id=1, replica_groups={{0,1,2,3},{4,5,6,7},{8,9,10,11},{12,13,14,15},{16,17,18,19},{20,21,22,2..., dimensions={0} | all-to-all | bytes 294912 | tf_op jit(solution)/shard_map/all_to_all | solution.py:210
  11.2 0.0 copy-start
  11.2 0.1 relay.1
  11.2 1.6 %collective-permute-start = (bf16[160,128]{1,0:T(8,128)(2,1)S(1)}, bf16[160,128]{1,0:T(8,128)(2,1)S(1)}, u32[]{:S(2)}, u32[]{:S(2)}) collective-permute-start(bf16[160,128]{1,0:T(8,128)(2,1)S(1)} %get-tuple-element.19), channel_id=1, source_target_pairs={{0,4},{1,5},{2,6},{3,7},{4,0},{5,1},{6,2},{7,3},{8,12},{9,13},{10,... | collective-permute-start | bytes 122888 | tf_op jit(solution)/shard_map/ppermute | solution.py:224
  12.8 0.3 %collective-permute-start.1 = (bf16[160,128]{1,0:T(8,128)(2,1)S(1)}, bf16[160,128]{1,0:T(8,128)(2,1)S(1)}, u32[]{:S(2)}, u32[]{:S(2)}) collective-permute-start(bf16[160,128]{1,0:T(8,128)(2,1)S(1)} %get-tuple-element.20), channel_id=1, source_target_pairs={{0,8},{1,9},{2,10},{3,11},{4,12},{5,13},{6,14},{7,15},{8,0},{9,1},... | collective-permute-start | bytes 122888 | tf_op jit(solution)/shard_map/ppermute | solution.py:224
  13.2 1.6 %collective-permute-start.2 = (bf16[160,128]{1,0:T(8,128)(2,1)S(1)}, bf16[160,128]{1,0:T(8,128)(2,1)S(1)}, u32[]{:S(2)}, u32[]{:S(2)}) collective-permute-start(bf16[160,128]{1,0:T(8,128)(2,1)S(1)} %get-tuple-element.21), channel_id=1, source_target_pairs={{0,12},{1,13},{2,14},{3,15},{4,8},{5,9},{6,10},{7,11},{8,4},{9,5},... | collective-permute-start | bytes 122888 | tf_op jit(solution)/shard_map/ppermute | solution.py:224
  14.8 0.5 %collective-permute-done.refs_1_ = bf16[160,128]{1,0:T(8,128)(2,1)S(1)} collective-permute-done((bf16[160,128]{1,0:T(8,128)(2,1)S(1)}, bf16[160,128]{1,0:T(8,128)(2,1)S(1)}, u32[]{:S(2)}, u32[]{:S(2)}) %collective-permute-start) | collective-permute-done | bytes 40992 | tf_op jit(solution)/shard_map/ppermute | solution.py:224
  15.3 2.5 %collective-permute-done.1.refs_2_ = bf16[160,128]{1,0:T(8,128)(2,1)S(1)} collective-permute-done((bf16[160,128]{1,0:T(8,128)(2,1)S(1)}, bf16[160,128]{1,0:T(8,128)(2,1)S(1)}, u32[]{:S(2)}, u32[]{:S(2)}) %collective-permute-start.1) | collective-permute-done | bytes 40992 | tf_op jit(solution)/shard_map/ppermute | solution.py:224
  17.7 1.0 %collective-permute-done.2.refs_3_ = bf16[160,128]{1,0:T(8,128)(2,1)S(1)} collective-permute-done((bf16[160,128]{1,0:T(8,128)(2,1)S(1)}, bf16[160,128]{1,0:T(8,128)(2,1)S(1)}, u32[]{:S(2)}, u32[]{:S(2)}) %collective-permute-start.2) | collective-permute-done | bytes 40992 | tf_op jit(solution)/shard_map/ppermute | solution.py:224
  18.7 0.0 copy-done
  18.7 0.0 copy-start.1
  18.7 0.3 %adapter_shares.1 = (f32[32,32]{1,0:T(8,128)S(1)}, f32[32,32]{1,0:T(8,128)S(1)}) custom-call(bf16[4,144,128]{2,1,0:T(8,128)(2,1)S(1)} %copy-done, bf16[160,128]{1,0:T(8,128)(2,1)S(1)} %get-tuple-element.18.refs_0_, bf16[160,128]{1,0:T(8,128)(2,1)S(1)} %collective-permute-done.refs_1_, bf16[160,128]{1,0:T(8,128)(2,1)S(1)} %collective-permute-done.1.refs_2_, ...), custom_call_target="tpu_custom_call" | custom-call | tf_op jit(solution)/shard_map/adapter_shares/pallas_call | solution.py:226
  19.1 5.7 %collective-permute-start.3 = (f32[32,32]{1,0:T(8,128)S(1)}, f32[32,32]{1,0:T(8,128)S(1)}, u32[]{:S(2)}, u32[]{:S(2)}) collective-permute-start(f32[32,32]{1,0:T(8,128)S(1)} %get-tuple-element.25), channel_id=1, source_target_pairs={{0,0},{1,2},{2,4},{3,6},{4,8},{5,10},{6,12},{7,14},{8,16},{9,18},{... | collective-permute-start | bytes 12296 | tf_op jit(solution)/shard_map/ppermute | solution.py:238
  24.8 0.1 collective-permute-start.4
  24.9 0.0 copy-done.1
  24.9 0.9 %owner_outputs.1 = (bf16[32,1024]{1,0:T(8,128)(2,1)}, bf16[32,1024]{1,0:T(8,128)(2,1)}, f32[32,32]{1,0:T(8,128)}) custom-call(bf16[32,1024]{1,0:T(8,128)(2,1)S(1)} %copy-done.1, bf16[160,128]{1,0:T(8,128)(2,1)S(1)} %get-tuple-element.18.refs_0_, bf16[160,128]{1,0:T(8,128)(2,1)S(1)} %collective-permute-done.refs_1_, ...), custom_call_target="tpu_custom_call" | custom-call | tf_op jit(solution)/shard_map/owner_outputs/pallas_call | solution.py:241
  25.7 0.5 %collective-permute-done.3 = f32[32,32]{1,0:T(8,128)S(1)} collective-permute-done((f32[32,32]{1,0:T(8,128)S(1)}, f32[32,32]{1,0:T(8,128)S(1)}, u32[]{:S(2)}, u32[]{:S(2)}) %collective-permute-start.3) | collective-permute-done | bytes 4128 | tf_op jit(solution)/shard_map/ppermute | solution.py:238
  26.2 3.3 %collective-permute-done.4 = f32[32,32]{1,0:T(8,128)S(1)} collective-permute-done((f32[32,32]{1,0:T(8,128)S(1)}, f32[32,32]{1,0:T(8,128)S(1)}, u32[]{:S(2)}, u32[]{:S(2)}) %collective-permute-start.4) | collective-permute-done | bytes 4128 | tf_op jit(solution)/shard_map/ppermute | solution.py:238
  29.5 0.6 %add.3 = f32[32,32]{1,0:T(8,128)} add(f32[32,32]{1,0:T(8,128)S(1)} %collective-permute-done.3, f32[32,32]{1,0:T(8,128)S(1)} %collective-permute-done.4) | non-fusion elementwise | flops 1024 | bytes 12288 | tf_op jit(solution)/shard_map/add | solution.py:239
Async XLA Ops:
  11.2 7.5 %copy-start = (bf16[4,144,128]{2,1,0:T(8,128)(2,1)S(1)}, bf16[4,144,128]{2,1,0:T(8,128)(2,1)}, u32[]{:S(2)}) copy-start(bf16[4,144,128]{2,1,0:T(8,128)(2,1)} %get-tuple-element.17.sent_ref) | copy-start | bytes 442372
  11.2 4.0 %collective-permute-start = (bf16[160,128]{1,0:T(8,128)(2,1)S(1)}, bf16[160,128]{1,0:T(8,128)(2,1)S(1)}, u32[]{:S(2)}, u32[]{:S(2)}) collective-permute-start(bf16[160,128]{1,0:T(8,128)(2,1)S(1)} %get-tuple-element.19), channel_id=1, source_target_pairs={{0,4},{1,5},{2,6},{3,7},{4,0},{5,1},{6,2},{7,3},{8,12},{9,13},{10,... | collective-permute-start | bytes 122888 | tf_op jit(solution)/shard_map/ppermute | solution.py:224
  12.8 4.9 %collective-permute-start.1 = (bf16[160,128]{1,0:T(8,128)(2,1)S(1)}, bf16[160,128]{1,0:T(8,128)(2,1)S(1)}, u32[]{:S(2)}, u32[]{:S(2)}) collective-permute-start(bf16[160,128]{1,0:T(8,128)(2,1)S(1)} %get-tuple-element.20), channel_id=1, source_target_pairs={{0,8},{1,9},{2,10},{3,11},{4,12},{5,13},{6,14},{7,15},{8,0},{9,1},... | collective-permute-start | bytes 122888 | tf_op jit(solution)/shard_map/ppermute | solution.py:224
  13.2 5.5 %collective-permute-start.2 = (bf16[160,128]{1,0:T(8,128)(2,1)S(1)}, bf16[160,128]{1,0:T(8,128)(2,1)S(1)}, u32[]{:S(2)}, u32[]{:S(2)}) collective-permute-start(bf16[160,128]{1,0:T(8,128)(2,1)S(1)} %get-tuple-element.21), channel_id=1, source_target_pairs={{0,12},{1,13},{2,14},{3,15},{4,8},{5,9},{6,10},{7,11},{8,4},{9,5},... | collective-permute-start | bytes 122888 | tf_op jit(solution)/shard_map/ppermute | solution.py:224
  18.7 6.1 %copy-start.1 = (bf16[32,1024]{1,0:T(8,128)(2,1)S(1)}, bf16[32,1024]{1,0:T(8,128)(2,1)}, u32[]{:S(2)}) copy-start(bf16[32,1024]{1,0:T(8,128)(2,1)} %up_ref.1) | copy-start | bytes 196612
  19.1 7.1 %collective-permute-start.3 = (f32[32,32]{1,0:T(8,128)S(1)}, f32[32,32]{1,0:T(8,128)S(1)}, u32[]{:S(2)}, u32[]{:S(2)}) collective-permute-start(f32[32,32]{1,0:T(8,128)S(1)} %get-tuple-element.25), channel_id=1, source_target_pairs={{0,0},{1,2},{2,4},{3,6},{4,8},{5,10},{6,12},{7,14},{8,16},{9,18},{... | collective-permute-start | bytes 12296 | tf_op jit(solution)/shard_map/ppermute | solution.py:238
  24.8 4.7 %collective-permute-start.4 = (f32[32,32]{1,0:T(8,128)S(1)}, f32[32,32]{1,0:T(8,128)S(1)}, u32[]{:S(2)}, u32[]{:S(2)}) collective-permute-start(f32[32,32]{1,0:T(8,128)S(1)} %get-tuple-element.26), channel_id=1, source_target_pairs={{0,1},{1,3},{2,5},{3,7},{4,9},{5,11},{6,13},{7,15},{8,17},{9,19},{... | collective-permute-start | bytes 12296 | tf_op jit(solution)/shard_map/ppermute | solution.py:238

commit v4 on v2

--- a/solution.py
+++ b/solution.py
@@ -37,18 +37,22 @@
     return first, last
 
 
-def attention_kernel(dp, mp, source_any, target_any, query_ref, grad_ref, kv_ref, *refs):
-    low_refs = refs[:dp]
-    query_grad_ref, both_grad_ref = refs[dp:dp + 2]
-    piece_refs = refs[dp + 2:dp + 2 + dp]
-    source_ref, target_ref, pieces, sems = refs[dp + 2 + dp:]
-    source_copy = pltpu.make_async_copy(source_any, source_ref, sems.at[0])
-    target_copy = pltpu.make_async_copy(target_any, target_ref, sems.at[1])
-    source_copy.start()
-    target_copy.start()
+def attention_kernel(
+    rows, source_any, target_any, query_any, grad_any, kv_any, query_grad_ref, both_grad_ref, *refs
+):
+    *piece_refs, source_ref, target_ref, query_ref, grad_ref, kv_ref, pieces, sems = refs
+    pairs = [
+        (kv_any, kv_ref), (query_any, query_ref), (grad_any, grad_ref),
+        (source_any, source_ref), (target_any, target_ref),
+    ]
+    copies = [
+        pltpu.make_async_copy(here, there, sems.at[i]) for i, (here, there) in enumerate(pairs)
+    ]
+    for copy in copies:
+        copy.start()
+    for copy in copies:
+        copy.wait()
     tgt_count = query_ref.shape[1]
-    src_count = kv_ref.shape[0]
-    rows = src_count // mp
     both = kv_ref[...]
     query_t = query_ref[...]
     grad_t = grad_ref[...]
@@ -57,8 +61,6 @@
     grad_wide = jnp.concatenate([blank, grad_t], axis=0)
     scores = jnp.dot(both, query_wide, preferred_element_type=jnp.float32)
     dprob = jnp.dot(both, grad_wide, preferred_element_type=jnp.float32)
-    source_copy.wait()
-    target_copy.wait()
     first, last = source_range(source_ref, target_ref, tgt_count)
     position = lax.broadcasted_iota(jnp.int32, scores.shape, 0)
     allowed = jnp.logical_and(position >= first, position < last)
@@ -70,28 +72,17 @@
     dscore = (prob * (dprob - delta)).astype(jnp.bfloat16)
     both_grad = dot(dscore, query_wide, NT) + dot(prob_low, grad_wide, NT)
     both_low = both_grad.astype(jnp.bfloat16)
-
-    both_rank = low_refs[0].shape[1]
+    blocks = both_grad_ref.shape[0]
+    for block in range(blocks):
+        both_grad_ref[block] = both_low[block * rows:(block + 1) * rows]
+
+    order = []
+    for start in range(0, rows, CUT):
+        for block in range(blocks):
+            order.append(both_low[block * rows + start:block * rows + start + CUT])
+    turned = jnp.concatenate(order, axis=0).astype(jnp.float32).T.astype(jnp.bfloat16)
     mine = lax.axis_index("dp")
-    parts = []
-    for low_ref in low_refs:
-        for cut in range(rows // CUT):
-            parts.append(low_ref[cut * CUT:(cut + 1) * CUT, :])
-    side = LANES // both_rank
-    packed = [
-        jnp.concatenate(parts[at:at + side], axis=1) for at in range(0, len(parts), side)
-    ]
-    packed = jnp.concatenate(packed, axis=0) if len(packed) > 1 else packed[0]
-    for block in range(mp):
-        both_grad_ref[block, :rows, :] = both_low[block * rows:(block + 1) * rows]
-        both_grad_ref[block, rows:, :] = packed
-
-    order = []
-    for cut in range(rows // CUT):
-        for block in range(mp):
-            start = block * rows + cut * CUT
-            order.append(both_low[start:start + CUT])
-    turned = jnp.concatenate(order, axis=0).astype(jnp.float32).T.astype(jnp.bfloat16)
+    dp = len(piece_refs)
     step = HS // dp
     for j in range(dp):
         pieces[j] = jnp.concatenate(
@@ -102,6 +93,25 @@
 
     query_grad = dot(both, dscore, TN)
     query_grad_ref[...] = query_grad[:HS].astype(jnp.bfloat16)
+
+
+def low_rank_kernel(rows, both_grad_ref, *refs):
+    *low_refs, out_ref = refs
+    mine = lax.axis_index("dp")
+    dp = len(low_refs)
+    both_rank = low_refs[0].shape[1]
+    side = LANES // both_rank
+    parts = []
+    for pack in range(dp):
+        low = low_refs[0][...]
+        for s in range(1, dp):
+            low = jnp.where(lax.rem(mine + dp - s, dp) == pack, low_refs[s][...], low)
+        parts.extend(low[at:at + CUT] for at in range(0, rows, CUT))
+    packed = [jnp.concatenate(parts[at:at + side], axis=1) for at in range(0, len(parts), side)]
+    for block in range(out_ref.shape[0]):
+        out_ref[block, :rows, :] = both_grad_ref[block]
+        for group, part in enumerate(packed):
+            out_ref[block, rows + group * CUT:rows + (group + 1) * CUT, :] = part
 
 
 def owner_kernel(dp, mp, got_ref, up_ref, *refs):
@@ -158,36 +168,46 @@
     vmem = pl.BlockSpec(memory_space=pltpu.VMEM)
     hbm = pl.BlockSpec(memory_space=pl.ANY)
     params = pltpu.CompilerParams(vmem_limit_bytes=48 * 1024 * 1024)
+    whole_vmem = pltpu.CompilerParams(vmem_limit_bytes=60 * 1024 * 1024)
 
     seen = [low_rank]
     for s in range(1, dp):
         seen.append(lax.ppermute(low_rank, "dp", [(d, (d + s) % dp) for d in range(dp)]))
-    mine = lax.axis_index("dp")
-    lows = []
-    for pack in range(dp):
-        low = seen[0]
-        for s in range(1, dp):
-            low = jnp.where((mine - s) % dp == pack, seen[s], low)
-        lows.append(low)
-
-    query_grad_t, sent, *pieces = pl.pallas_call(
-        functools.partial(attention_kernel, dp, mp),
+
+    query_t = query.T
+    grad_t = out_grad.T
+    query_grad_t, both_grad, *pieces = pl.pallas_call(
+        functools.partial(attention_kernel, rows),
         out_shape=[
             jax.ShapeDtypeStruct((HS, tgt_count), jnp.bfloat16),
-            jax.ShapeDtypeStruct((mp, rows + low_rows, LANES), jnp.bfloat16),
+            jax.ShapeDtypeStruct((mp, rows, LANES), jnp.bfloat16),
         ] + [jax.ShapeDtypeStruct((2 * step, src_count), jnp.bfloat16)] * dp,
-        in_specs=[hbm, hbm] + [vmem] * (3 + dp),
+        in_specs=[hbm] * 5,
         out_specs=[vmem] * (2 + dp),
         scratch_shapes=[
             pltpu.SMEM(source_lengths.shape, jnp.int32),
             pltpu.SMEM(target_lengths.shape, jnp.int32),
+            pltpu.VMEM(query_t.shape, jnp.bfloat16),
+            pltpu.VMEM(grad_t.shape, jnp.bfloat16),
+            pltpu.VMEM(kv_cache.shape, jnp.bfloat16),
             pltpu.VMEM((dp, 2 * step, src_count), jnp.bfloat16),
-            pltpu.SemaphoreType.DMA((2,)),
+            pltpu.SemaphoreType.DMA((5,)),
         ],
+        compiler_params=whole_vmem,
+        cost_estimate=pl.CostEstimate(
+            flops=10 * tgt_count * src_count * 2 * HS, bytes_accessed=2 ** 23, transcendentals=0
+        ),
+        name="attention_backward",
+    )(source_lengths, target_lengths, query_t, grad_t, kv_cache)
+
+    sent = pl.pallas_call(
+        functools.partial(low_rank_kernel, rows),
+        out_shape=jax.ShapeDtypeStruct((mp, rows + low_rows, LANES), jnp.bfloat16),
+        in_specs=[vmem] * (1 + dp),
+        out_specs=vmem,
         compiler_params=params,
-        name="attention_backward",
-    )(source_lengths, target_lengths, query.T, out_grad.T, kv_cache, *lows)
-
+        name="low_rank_rows",
+    )(both_grad, *seen)
     got = lax.all_to_all(sent, "mp", split_axis=0, concat_axis=0, tiled=True)
 
     arrived = []

time: 26.5 us -> 24.7 us (0.932)
  the two profiles are of different devices: /device:TPU:4 before, /device:TPU:5 now
where the time goes in v4:
time: 24.7 us; the launch traced here: 24.5 us
  starting transfers between devices  13 us (53%)
  waiting for transfers between devices  5.56 us (23%)
  Pallas kernels  4.26 us (17%)
  local copies, waits for them, and re-layouts  0.92 us (4%)
  between operations  0.68 us (3%)
    all_to_all x1, starting transfers between devices, local(): got = lax.all_to_all(sent, 'mp', split_axis=0, concat_axis=0, tiled=True)  7.77 us
    ppermute x2, waiting for transfers between devices, local(): arrived.append(lax.ppermute(pieces[s], ('dp', 'mp'), route))  5.37 us
    ppermute x2, starting transfers between devices, local(): arrived.append(lax.ppermute(pieces[s], ('dp', 'mp'), route))  5.19 us
    pallas_call x1, Pallas kernels, local(): pl.pallas_call(functools.partial(attention_kernel, rows), out_shape=[jax....  2.5 us
    pallas_call x1, Pallas kernels, local(): pl.pallas_call(functools.partial(owner_kernel, dp, mp), out_shape=[jax.Sh...  0.99 us
    unnamed x10, local copies, waits for them, and re-layouts  0.92 us
    pallas_call x1, Pallas kernels, local(): pl.pallas_call(functools.partial(low_rank_kernel, rows), out_shape=jax.Sh...  0.77 us
  transfers between devices with their start and end apart: 4, of which 3 were waited for; matrix products, arithmetic and copies ran while one was open for 0% of the time, Pallas kernels for 10%

profile of v4, /device:TPU:5, one launch (start us, length us, event | category | flops | bytes accessed | tf_op | source)
XLA Modules:
  0.0 24.5 jit_solution(12762746986785344259)
XLA Ops:
  0.6 0.1 collective-permute-start
  0.7 0.0 copy-start.2
  0.7 2.5 %attention_backward.1 = (bf16[64,256]{1,0:T(8,128)(2,1)}, bf16[16,32,128]{2,1,0:T(8,128)(2,1)}, bf16[64,512]{1,0:T(8,128)(2,1)}, bf16[64,512]{1,0:T(8,128)(2,1)}) custom-call(s32[1,8]{1,0:T(1,128)} %source_any.1, s32[1,8]{1,0:T(1,128)} %target_any.1, bf16[64,256]{1,0:T(8,128)(2,1)} %bitcast.3, bf16[64,256]{1,0:T(8,128)(2,1)} %bitcast.4, bf16[512,128]{1,0:T(8,128)(2,1)} %kv_any.1), custom_call_target="tpu_custom_call" | custom-call | flops 167772160 | bytes 8388608 | tf_op jit(solution)/shard_map/attention_backward/pallas_call | solution.py:179
  3.2 0.2 collective-permute-done.refs_1_
  3.4 0.0 copy-done.2
  3.4 0.0 copy-start
  3.4 0.9 %copy-done = bf16[16,32,128]{2,1,0:T(8,128)(2,1)S(1)} copy-done((bf16[16,32,128]{2,1,0:T(8,128)(2,1)S(1)}, bf16[16,32,128]{2,1,0:T(8,128)(2,1)}, u32[]{:S(2)}) %copy-start) | copy-done | bytes 131096
  4.3 0.8 %low_rank_rows.1 = bf16[16,48,128]{2,1,0:T(8,128)(2,1)} custom-call(bf16[16,32,128]{2,1,0:T(8,128)(2,1)S(1)} %copy-done, bf16[32,32]{1,0:T(8,128)(2,1)S(1)} %copy-done.2, bf16[32,32]{1,0:T(8,128)(2,1)S(1)} %collective-permute-done.refs_1_), custom_call_target="tpu_custom_call" | custom-call | tf_op jit(solution)/shard_map/low_rank_rows/pallas_call | solution.py:203
  5.1 0.0 copy-start.4
  5.1 0.0 copy-start.3
  5.1 0.0 copy-start.1
  5.1 7.8 %all-to-all-start = ((bf16[16,48,128]{2,1,0:T(8,128)(2,1)}), bf16[16,48,128]{2,1,0:T(8,128)(2,1)S(1)}, u32[]{:S(2)}, u32[]{:S(2)}) async-start(bf16[16,48,128]{2,1,0:T(8,128)(2,1)} %low_rank_rows.1), calls=%async_computation | async-start | bytes 393216 | tf_op jit(solution)/shard_map/all_to_all | solution.py:211
  12.9 0.0 copy-done.4
  12.9 3.4 %collective-permute-start.1 = (bf16[64,512]{1,0:T(8,128)(2,1)S(1)}, bf16[64,512]{1,0:T(8,128)(2,1)S(1)}, u32[]{:S(2)}, u32[]{:S(2)}) collective-permute-start(bf16[64,512]{1,0:T(8,128)(2,1)S(1)} %copy-done.4), channel_id=1, source_target_pairs={{0,0},{1,2},{2,4},{3,6},{4,8},{5,10},{6,12},{7,14},{8,16},{9,18},{... | collective-permute-start | bytes 196616 | tf_op jit(solution)/shard_map/ppermute | solution.py:216
  16.3 0.0 copy-done.3
  16.3 1.8 %collective-permute-start.2 = (bf16[64,512]{1,0:T(8,128)(2,1)S(1)}, bf16[64,512]{1,0:T(8,128)(2,1)S(1)}, u32[]{:S(2)}, u32[]{:S(2)}) collective-permute-start(bf16[64,512]{1,0:T(8,128)(2,1)S(1)} %copy-done.3), channel_id=1, source_target_pairs={{0,1},{1,3},{2,5},{3,7},{4,9},{5,11},{6,13},{7,15},{8,17},{9,19},{... | collective-permute-start | bytes 196616 | tf_op jit(solution)/shard_map/ppermute | solution.py:216
  18.1 4.5 %collective-permute-done.1.refs_0_ = bf16[64,512]{1,0:T(8,128)(2,1)S(1)} collective-permute-done((bf16[64,512]{1,0:T(8,128)(2,1)S(1)}, bf16[64,512]{1,0:T(8,128)(2,1)S(1)}, u32[]{:S(2)}, u32[]{:S(2)}) %collective-permute-start.1) | collective-permute-done | bytes 65568 | tf_op jit(solution)/shard_map/ppermute | solution.py:216
  22.6 0.9 %collective-permute-done.2.refs_1_ = bf16[64,512]{1,0:T(8,128)(2,1)S(1)} collective-permute-done((bf16[64,512]{1,0:T(8,128)(2,1)S(1)}, bf16[64,512]{1,0:T(8,128)(2,1)S(1)}, u32[]{:S(2)}, u32[]{:S(2)}) %collective-permute-start.2) | collective-permute-done | bytes 65568 | tf_op jit(solution)/shard_map/ppermute | solution.py:216
  23.5 0.0 all-to-all-done.got_ref
  23.5 0.0 copy-done.1
  23.5 1.0 %owner_outputs.1 = (bf16[32,1024]{1,0:T(8,128)(2,1)}, bf16[32,1024]{1,0:T(8,128)(2,1)}, f32[32,32]{1,0:T(8,128)}, f32[32,32]{1,0:T(8,128)}) custom-call(bf16[16,48,128]{2,1,0:T(8,128)(2,1)S(1)} %all-to-all-done.got_ref, bf16[32,1024]{1,0:T(8,128)(2,1)S(1)} %copy-done.1, bf16[64,512]{1,0:T(8,128)(2,1)S(1)} %collective-permute-done.1.refs_0_, ...), custom_call_target="tpu_custom_call" | custom-call | tf_op jit(solution)/shard_map/owner_outputs/pallas_call | solution.py:218
Async XLA Ops:
  0.6 2.8 %collective-permute-start = (bf16[32,32]{1,0:T(8,128)(2,1)}, bf16[32,32]{1,0:T(8,128)(2,1)S(1)}, u32[]{:S(2)}, u32[]{:S(2)}) collective-permute-start(bf16[32,32]{1,0:T(8,128)(2,1)} %refs_0_.1), channel_id=1, source_target_pairs={{0,16},{16,0},{1,17},{17,1},{2,18},{18,2},{3,19},{19,3},{4,20},{20... | collective-permute-start | bytes 6152 | tf_op jit(solution)/shard_map/ppermute | solution.py:175
  0.7 2.7 %copy-start.2 = (bf16[32,32]{1,0:T(8,128)(2,1)S(1)}, bf16[32,32]{1,0:T(8,128)(2,1)}, u32[]{:S(2)}) copy-start(bf16[32,32]{1,0:T(8,128)(2,1)} %refs_0_.1) | copy-start | bytes 6148
  3.4 0.9 %copy-start = (bf16[16,32,128]{2,1,0:T(8,128)(2,1)S(1)}, bf16[16,32,128]{2,1,0:T(8,128)(2,1)}, u32[]{:S(2)}) copy-start(bf16[16,32,128]{2,1,0:T(8,128)(2,1)} %get-tuple-element.14.both_grad_ref) | copy-start | bytes 393220
  5.1 7.8 %copy-start.4 = (bf16[64,512]{1,0:T(8,128)(2,1)S(1)}, bf16[64,512]{1,0:T(8,128)(2,1)}, u32[]{:S(2)}) copy-start(bf16[64,512]{1,0:T(8,128)(2,1)} %get-tuple-element.15) | copy-start | bytes 196612
  5.1 11.2 %copy-start.3 = (bf16[64,512]{1,0:T(8,128)(2,1)S(1)}, bf16[64,512]{1,0:T(8,128)(2,1)}, u32[]{:S(2)}) copy-start(bf16[64,512]{1,0:T(8,128)(2,1)} %get-tuple-element.16) | copy-start | bytes 196612
  5.1 18.4 %copy-start.1 = (bf16[32,1024]{1,0:T(8,128)(2,1)S(1)}, bf16[32,1024]{1,0:T(8,128)(2,1)}, u32[]{:S(2)}) copy-start(bf16[32,1024]{1,0:T(8,128)(2,1)} %up_ref.1) | copy-start | bytes 196612
  5.1 18.4 %all-to-all-start = ((bf16[16,48,128]{2,1,0:T(8,128)(2,1)}), bf16[16,48,128]{2,1,0:T(8,128)(2,1)S(1)}, u32[]{:S(2)}, u32[]{:S(2)}) async-start(bf16[16,48,128]{2,1,0:T(8,128)(2,1)} %low_rank_rows.1), calls=%async_computation | async-start | bytes 393216 | tf_op jit(solution)/shard_map/all_to_all | solution.py:211
  12.9 9.7 %collective-permute-start.1 = (bf16[64,512]{1,0:T(8,128)(2,1)S(1)}, bf16[64,512]{1,0:T(8,128)(2,1)S(1)}, u32[]{:S(2)}, u32[]{:S(2)}) collective-permute-start(bf16[64,512]{1,0:T(8,128)(2,1)S(1)} %copy-done.4), channel_id=1, source_target_pairs={{0,0},{1,2},{2,4},{3,6},{4,8},{5,10},{6,12},{7,14},{8,16},{9,18},{... | collective-permute-start | bytes 196616 | tf_op jit(solution)/shard_map/ppermute | solution.py:216
  16.3 7.1 %collective-permute-start.2 = (bf16[64,512]{1,0:T(8,128)(2,1)S(1)}, bf16[64,512]{1,0:T(8,128)(2,1)S(1)}, u32[]{:S(2)}, u32[]{:S(2)}) collective-permute-start(bf16[64,512]{1,0:T(8,128)(2,1)S(1)} %copy-done.3), channel_id=1, source_target_pairs={{0,1},{1,3},{2,5},{3,7},{4,9},{5,11},{6,13},{7,15},{8,17},{9,19},{... | collective-permute-start | bytes 196616 | tf_op jit(solution)/shard_map/ppermute | solution.py:216

commit v5 on v4

--- a/solution.py
+++ b/solution.py
@@ -19,6 +19,12 @@
 
 def dot(left, right, dims):
     return lax.dot_general(left, right, dims, preferred_element_type=jnp.float32)
+
+
+def spread_order(count):
+    bits = count.bit_length() - 1
+    assert count == 1 << bits
+    return [sum(((i >> b) & 1) << (bits - 1 - b) for b in range(bits)) for i in range(count)]
 
 
 def source_range(source_ref, target_ref, count):
@@ -73,8 +79,8 @@
     both_grad = dot(dscore, query_wide, NT) + dot(prob_low, grad_wide, NT)
     both_low = both_grad.astype(jnp.bfloat16)
     blocks = both_grad_ref.shape[0]
-    for block in range(blocks):
-        both_grad_ref[block] = both_low[block * rows:(block + 1) * rows]
+    for at, block in enumerate(spread_order(blocks)):
+        both_grad_ref[at] = both_low[block * rows:(block + 1) * rows]
 
     order = []
     for start in range(0, rows, CUT):
@@ -120,9 +126,10 @@
     rows = key_ref.shape[0]
     both_rank = up_ref.shape[0]
     rank = both_rank // 2
+    places = spread_order(mp)
     for pair in range(mp // 2):
-        first = got_ref[2 * pair, :rows, :]
-        second = got_ref[2 * pair + 1, :rows, :]
+        first = got_ref[places.index(2 * pair), :rows, :]
+        second = got_ref[places.index(2 * pair + 1), :rows, :]
         columns = slice(2 * pair * HS, (2 * pair + 2) * HS)
         key_ref[:, columns] = jnp.concatenate([first[:, :HS], second[:, :HS]], axis=1)
         value_ref[:, columns] = jnp.concatenate([first[:, HS:], second[:, HS:]], axis=1)
@@ -142,7 +149,7 @@
     lows = []
     for group in range(dp * cuts // side):
         at = rows + group * CUT
-        lows.append(jnp.concatenate([got_ref[block, at:at + CUT, :] for block in range(mp)], axis=0))
+        lows.append(jnp.concatenate([got_ref[place, at:at + CUT, :] for place in places], axis=0))
     for s in range(dp):
         pack = lax.rem(lax.rem(me, dp) + dp - s, dp)
         for cut in range(cuts):
@@ -208,7 +215,9 @@
         compiler_params=params,
         name="low_rank_rows",
     )(both_grad, *seen)
-    got = lax.all_to_all(sent, "mp", split_axis=0, concat_axis=0, tiled=True)
+    got = lax.all_to_all(
+        sent, "mp", split_axis=0, concat_axis=0, axis_index_groups=[spread_order(mp)], tiled=True
+    )
 
     arrived = []
     for s in range(dp):

time: 24.7 us -> 24.7 us (level)
  no operation moved by 1% of the time
where the time goes in v5:
time: 24.7 us; the launch traced here: 24.5 us
  starting transfers between devices  13 us (53%)
  waiting for transfers between devices  5.56 us (23%)
  Pallas kernels  4.26 us (17%)
  local copies, waits for them, and re-layouts  0.92 us (4%)
  between operations  0.68 us (3%)
    all_to_all x1, starting transfers between devices, local(): lax.all_to_all(sent, 'mp', split_axis=0, concat_axis=0, axis_index_groups...  7.78 us
    ppermute x2, waiting for transfers between devices, local(): arrived.append(lax.ppermute(pieces[s], ('dp', 'mp'), route))  5.37 us
    ppermute x2, starting transfers between devices, local(): arrived.append(lax.ppermute(pieces[s], ('dp', 'mp'), route))  5.19 us
    pallas_call x1, Pallas kernels, local(): pl.pallas_call(functools.partial(attention_kernel, rows), out_shape=[jax....  2.5 us
    pallas_call x1, Pallas kernels, local(): pl.pallas_call(functools.partial(owner_kernel, dp, mp), out_shape=[jax.Sh...  0.99 us
    unnamed x10, local copies, waits for them, and re-layouts  0.92 us
    pallas_call x1, Pallas kernels, local(): pl.pallas_call(functools.partial(low_rank_kernel, rows), out_shape=jax.Sh...  0.77 us
  transfers between devices with their start and end apart: 4, of which 3 were waited for; matrix products, arithmetic and copies ran while one was open for 0% of the time, Pallas kernels for 10%

profile of v5, /device:TPU:5, one launch (start us, length us, event | category | flops | bytes accessed | tf_op | source)
XLA Modules:
  0.0 24.5 jit_solution(9944236110156125318)
XLA Ops:
  0.6 0.1 collective-permute-start
  0.7 0.0 copy-start.2
  0.7 2.5 %attention_backward.1 = (bf16[64,256]{1,0:T(8,128)(2,1)}, bf16[16,32,128]{2,1,0:T(8,128)(2,1)}, bf16[64,512]{1,0:T(8,128)(2,1)}, bf16[64,512]{1,0:T(8,128)(2,1)}) custom-call(s32[1,8]{1,0:T(1,128)} %source_any.1, s32[1,8]{1,0:T(1,128)} %target_any.1, bf16[64,256]{1,0:T(8,128)(2,1)} %bitcast.3, bf16[64,256]{1,0:T(8,128)(2,1)} %bitcast.4, bf16[512,128]{1,0:T(8,128)(2,1)} %kv_any.1), custom_call_target="tpu_custom_call" | custom-call | flops 167772160 | bytes 8388608 | tf_op jit(solution)/shard_map/attention_backward/pallas_call | solution.py:186
  3.2 0.2 collective-permute-done.refs_1_
  3.4 0.0 copy-done.2
  3.4 0.0 copy-start
  3.4 0.9 %copy-done = bf16[16,32,128]{2,1,0:T(8,128)(2,1)S(1)} copy-done((bf16[16,32,128]{2,1,0:T(8,128)(2,1)S(1)}, bf16[16,32,128]{2,1,0:T(8,128)(2,1)}, u32[]{:S(2)}) %copy-start) | copy-done | bytes 131096
  4.3 0.8 %low_rank_rows.1 = bf16[16,48,128]{2,1,0:T(8,128)(2,1)} custom-call(bf16[16,32,128]{2,1,0:T(8,128)(2,1)S(1)} %copy-done, bf16[32,32]{1,0:T(8,128)(2,1)S(1)} %copy-done.2, bf16[32,32]{1,0:T(8,128)(2,1)S(1)} %collective-permute-done.refs_1_), custom_call_target="tpu_custom_call" | custom-call | tf_op jit(solution)/shard_map/low_rank_rows/pallas_call | solution.py:210
  5.1 0.0 copy-start.4
  5.1 0.0 copy-start.3
  5.1 0.0 copy-start.1
  5.1 7.8 %all-to-all-start = ((bf16[16,48,128]{2,1,0:T(8,128)(2,1)}), bf16[16,48,128]{2,1,0:T(8,128)(2,1)S(1)}, u32[]{:S(2)}, u32[]{:S(2)}) async-start(bf16[16,48,128]{2,1,0:T(8,128)(2,1)} %low_rank_rows.1), calls=%async_computation | async-start | bytes 393216 | tf_op jit(solution)/shard_map/all_to_all | solution.py:218
  12.9 0.0 copy-done.4
  12.9 3.4 %collective-permute-start.1 = (bf16[64,512]{1,0:T(8,128)(2,1)S(1)}, bf16[64,512]{1,0:T(8,128)(2,1)S(1)}, u32[]{:S(2)}, u32[]{:S(2)}) collective-permute-start(bf16[64,512]{1,0:T(8,128)(2,1)S(1)} %copy-done.4), channel_id=1, source_target_pairs={{0,0},{1,2},{2,4},{3,6},{4,8},{5,10},{6,12},{7,14},{8,16},{9,18},{... | collective-permute-start | bytes 196616 | tf_op jit(solution)/shard_map/ppermute | solution.py:225
  16.3 0.0 copy-done.3
  16.3 1.8 %collective-permute-start.2 = (bf16[64,512]{1,0:T(8,128)(2,1)S(1)}, bf16[64,512]{1,0:T(8,128)(2,1)S(1)}, u32[]{:S(2)}, u32[]{:S(2)}) collective-permute-start(bf16[64,512]{1,0:T(8,128)(2,1)S(1)} %copy-done.3), channel_id=1, source_target_pairs={{0,1},{1,3},{2,5},{3,7},{4,9},{5,11},{6,13},{7,15},{8,17},{9,19},{... | collective-permute-start | bytes 196616 | tf_op jit(solution)/shard_map/ppermute | solution.py:225
  18.1 4.5 %collective-permute-done.1.refs_0_ = bf16[64,512]{1,0:T(8,128)(2,1)S(1)} collective-permute-done((bf16[64,512]{1,0:T(8,128)(2,1)S(1)}, bf16[64,512]{1,0:T(8,128)(2,1)S(1)}, u32[]{:S(2)}, u32[]{:S(2)}) %collective-permute-start.1) | collective-permute-done | bytes 65568 | tf_op jit(solution)/shard_map/ppermute | solution.py:225
  22.6 0.9 %collective-permute-done.2.refs_1_ = bf16[64,512]{1,0:T(8,128)(2,1)S(1)} collective-permute-done((bf16[64,512]{1,0:T(8,128)(2,1)S(1)}, bf16[64,512]{1,0:T(8,128)(2,1)S(1)}, u32[]{:S(2)}, u32[]{:S(2)}) %collective-permute-start.2) | collective-permute-done | bytes 65568 | tf_op jit(solution)/shard_map/ppermute | solution.py:225
  23.5 0.0 all-to-all-done.got_ref
  23.5 0.0 copy-done.1
  23.5 1.0 %owner_outputs.1 = (bf16[32,1024]{1,0:T(8,128)(2,1)}, bf16[32,1024]{1,0:T(8,128)(2,1)}, f32[32,32]{1,0:T(8,128)}, f32[32,32]{1,0:T(8,128)}) custom-call(bf16[16,48,128]{2,1,0:T(8,128)(2,1)S(1)} %all-to-all-done.got_ref, bf16[32,1024]{1,0:T(8,128)(2,1)S(1)} %copy-done.1, bf16[64,512]{1,0:T(8,128)(2,1)S(1)} %collective-permute-done.1.refs_0_, ...), custom_call_target="tpu_custom_call" | custom-call | tf_op jit(solution)/shard_map/owner_outputs/pallas_call | solution.py:227
Async XLA Ops:
  0.6 2.8 %collective-permute-start = (bf16[32,32]{1,0:T(8,128)(2,1)}, bf16[32,32]{1,0:T(8,128)(2,1)S(1)}, u32[]{:S(2)}, u32[]{:S(2)}) collective-permute-start(bf16[32,32]{1,0:T(8,128)(2,1)} %refs_0_.1), channel_id=1, source_target_pairs={{0,16},{16,0},{1,17},{17,1},{2,18},{18,2},{3,19},{19,3},{4,20},{20... | collective-permute-start | bytes 6152 | tf_op jit(solution)/shard_map/ppermute | solution.py:182
  0.7 2.7 %copy-start.2 = (bf16[32,32]{1,0:T(8,128)(2,1)S(1)}, bf16[32,32]{1,0:T(8,128)(2,1)}, u32[]{:S(2)}) copy-start(bf16[32,32]{1,0:T(8,128)(2,1)} %refs_0_.1) | copy-start | bytes 6148
  3.4 0.9 %copy-start = (bf16[16,32,128]{2,1,0:T(8,128)(2,1)S(1)}, bf16[16,32,128]{2,1,0:T(8,128)(2,1)}, u32[]{:S(2)}) copy-start(bf16[16,32,128]{2,1,0:T(8,128)(2,1)} %get-tuple-element.14.both_grad_ref) | copy-start | bytes 393220
  5.1 7.8 %copy-start.4 = (bf16[64,512]{1,0:T(8,128)(2,1)S(1)}, bf16[64,512]{1,0:T(8,128)(2,1)}, u32[]{:S(2)}) copy-start(bf16[64,512]{1,0:T(8,128)(2,1)} %get-tuple-element.15) | copy-start | bytes 196612
  5.1 11.2 %copy-start.3 = (bf16[64,512]{1,0:T(8,128)(2,1)S(1)}, bf16[64,512]{1,0:T(8,128)(2,1)}, u32[]{:S(2)}) copy-start(bf16[64,512]{1,0:T(8,128)(2,1)} %get-tuple-element.16) | copy-start | bytes 196612
  5.1 18.4 %copy-start.1 = (bf16[32,1024]{1,0:T(8,128)(2,1)S(1)}, bf16[32,1024]{1,0:T(8,128)(2,1)}, u32[]{:S(2)}) copy-start(bf16[32,1024]{1,0:T(8,128)(2,1)} %up_ref.1) | copy-start | bytes 196612
  5.1 18.4 %all-to-all-start = ((bf16[16,48,128]{2,1,0:T(8,128)(2,1)}), bf16[16,48,128]{2,1,0:T(8,128)(2,1)S(1)}, u32[]{:S(2)}, u32[]{:S(2)}) async-start(bf16[16,48,128]{2,1,0:T(8,128)(2,1)} %low_rank_rows.1), calls=%async_computation | async-start | bytes 393216 | tf_op jit(solution)/shard_map/all_to_all | solution.py:218
  12.9 9.7 %collective-permute-start.1 = (bf16[64,512]{1,0:T(8,128)(2,1)S(1)}, bf16[64,512]{1,0:T(8,128)(2,1)S(1)}, u32[]{:S(2)}, u32[]{:S(2)}) collective-permute-start(bf16[64,512]{1,0:T(8,128)(2,1)S(1)} %copy-done.4), channel_id=1, source_target_pairs={{0,0},{1,2},{2,4},{3,6},{4,8},{5,10},{6,12},{7,14},{8,16},{9,18},{... | collective-permute-start | bytes 196616 | tf_op jit(solution)/shard_map/ppermute | solution.py:225
  16.3 7.1 %collective-permute-start.2 = (bf16[64,512]{1,0:T(8,128)(2,1)S(1)}, bf16[64,512]{1,0:T(8,128)(2,1)S(1)}, u32[]{:S(2)}, u32[]{:S(2)}) collective-permute-start(bf16[64,512]{1,0:T(8,128)(2,1)S(1)} %copy-done.3), channel_id=1, source_target_pairs={{0,1},{1,3},{2,5},{3,7},{4,9},{5,11},{6,13},{7,15},{8,17},{9,19},{... | collective-permute-start | bytes 196616 | tf_op jit(solution)/shard_map/ppermute | solution.py:225

commit v6 on v5

--- a/solution.py
+++ b/solution.py
@@ -21,10 +21,18 @@
     return lax.dot_general(left, right, dims, preferred_element_type=jnp.float32)
 
 
-def spread_order(count):
-    bits = count.bit_length() - 1
-    assert count == 1 << bits
-    return [sum(((i >> b) & 1) << (bits - 1 - b) for b in range(bits)) for i in range(count)]
+def group_order(count):
+    quarter = count // 4
+    bits = quarter.bit_length() - 1
+    assert count == 4 << bits
+    turned = [sum(((i >> b) & 1) << (bits - 1 - b) for b in range(bits)) for i in range(quarter)]
+    order = []
+    for low, high in ((1, 2), (0, 3)):
+        for i in range(0, quarter, 2):
+            first, second = turned[i], turned[i + 1]
+            order += [low * quarter + first, high * quarter + second]
+            order += [low * quarter + second, high * quarter + first]
+    return order
 
 
 def source_range(source_ref, target_ref, count):
@@ -79,7 +87,7 @@
     both_grad = dot(dscore, query_wide, NT) + dot(prob_low, grad_wide, NT)
     both_low = both_grad.astype(jnp.bfloat16)
     blocks = both_grad_ref.shape[0]
-    for at, block in enumerate(spread_order(blocks)):
+    for at, block in enumerate(group_order(blocks)):
         both_grad_ref[at] = both_low[block * rows:(block + 1) * rows]
 
     order = []
@@ -126,10 +134,11 @@
     rows = key_ref.shape[0]
     both_rank = up_ref.shape[0]
     rank = both_rank // 2
-    places = spread_order(mp)
+    order = group_order(mp)
+    places = [order.index(block) for block in range(mp)]
     for pair in range(mp // 2):
-        first = got_ref[places.index(2 * pair), :rows, :]
-        second = got_ref[places.index(2 * pair + 1), :rows, :]
+        first = got_ref[places[2 * pair], :rows, :]
+        second = got_ref[places[2 * pair + 1], :rows, :]
         columns = slice(2 * pair * HS, (2 * pair + 2) * HS)
         key_ref[:, columns] = jnp.concatenate([first[:, :HS], second[:, :HS]], axis=1)
         value_ref[:, columns] = jnp.concatenate([first[:, HS:], second[:, HS:]], axis=1)
@@ -216,7 +225,7 @@
         name="low_rank_rows",
     )(both_grad, *seen)
     got = lax.all_to_all(
-        sent, "mp", split_axis=0, concat_axis=0, axis_index_groups=[spread_order(mp)], tiled=True
+        sent, "mp", split_axis=0, concat_axis=0, axis_index_groups=[group_order(mp)], tiled=True
     )
 
     arrived = []

time: 24.7 us -> 24.1 us (0.976)
  the two profiles are of different devices: /device:TPU:5 before, /device:TPU:7 now
where the time goes in v6:
time: 24.1 us; the launch traced here: 23.8 us
  starting transfers between devices  13.2 us (55%)
  waiting for transfers between devices  4.73 us (20%)
  Pallas kernels  4.27 us (18%)
  local copies, waits for them, and re-layouts  0.91 us (4%)
  between operations  0.69 us (3%)
    all_to_all x1, starting transfers between devices, local(): lax.all_to_all(sent, 'mp', split_axis=0, concat_axis=0, axis_index_groups...  7.91 us
    ppermute x2, starting transfers between devices, local(): arrived.append(lax.ppermute(pieces[s], ('dp', 'mp'), route))  4.99 us
    ppermute x2, waiting for transfers between devices, local(): arrived.append(lax.ppermute(pieces[s], ('dp', 'mp'), route))  4.73 us
    pallas_call x1, Pallas kernels, local(): pl.pallas_call(functools.partial(attention_kernel, rows), out_shape=[jax....  2.5 us
    pallas_call x1, Pallas kernels, local(): pl.pallas_call(functools.partial(owner_kernel, dp, mp), out_shape=[jax.Sh...  0.99 us
    unnamed x10, local copies, waits for them, and re-layouts  0.91 us
    pallas_call x1, Pallas kernels, local(): pl.pallas_call(functools.partial(low_rank_kernel, rows), out_shape=jax.Sh...  0.77 us
  transfers between devices with their start and end apart: 4, of which 2 were waited for; matrix products, arithmetic and copies ran while one was open for 0% of the time, Pallas kernels for 11%

profile of v6, /device:TPU:7, one launch (start us, length us, event | category | flops | bytes accessed | tf_op | source)
XLA Modules:
  0.0 23.8 jit_solution(18128374626583664295)
XLA Ops:
  0.6 0.3 %collective-permute-start = (bf16[32,32]{1,0:T(8,128)(2,1)}, bf16[32,32]{1,0:T(8,128)(2,1)S(1)}, u32[]{:S(2)}, u32[]{:S(2)}) collective-permute-start(bf16[32,32]{1,0:T(8,128)(2,1)} %refs_0_.1), channel_id=1, source_target_pairs={{0,16},{16,0},{1,17},{17,1},{2,18},{18,2},{3,19},{19,3},{4,20},{20... | collective-permute-start | bytes 6152 | tf_op jit(solution)/shard_map/ppermute | solution.py:191
  0.9 0.0 copy-start.2
  0.9 2.5 %attention_backward.1 = (bf16[64,256]{1,0:T(8,128)(2,1)}, bf16[16,32,128]{2,1,0:T(8,128)(2,1)}, bf16[64,512]{1,0:T(8,128)(2,1)}, bf16[64,512]{1,0:T(8,128)(2,1)}) custom-call(s32[1,8]{1,0:T(1,128)} %source_any.1, s32[1,8]{1,0:T(1,128)} %target_any.1, bf16[64,256]{1,0:T(8,128)(2,1)} %bitcast.3, bf16[64,256]{1,0:T(8,128)(2,1)} %bitcast.4, bf16[512,128]{1,0:T(8,128)(2,1)} %kv_any.1), custom_call_target="tpu_custom_call" | custom-call | flops 167772160 | bytes 8388608 | tf_op jit(solution)/shard_map/attention_backward/pallas_call | solution.py:195
  3.4 0.0 collective-permute-done.refs_1_
  3.4 0.0 copy-done.2
  3.5 0.0 copy-start
  3.5 0.9 %copy-done = bf16[16,32,128]{2,1,0:T(8,128)(2,1)S(1)} copy-done((bf16[16,32,128]{2,1,0:T(8,128)(2,1)S(1)}, bf16[16,32,128]{2,1,0:T(8,128)(2,1)}, u32[]{:S(2)}) %copy-start) | copy-done | bytes 131096
  4.4 0.8 %low_rank_rows.1 = bf16[16,48,128]{2,1,0:T(8,128)(2,1)} custom-call(bf16[16,32,128]{2,1,0:T(8,128)(2,1)S(1)} %copy-done, bf16[32,32]{1,0:T(8,128)(2,1)S(1)} %copy-done.2, bf16[32,32]{1,0:T(8,128)(2,1)S(1)} %collective-permute-done.refs_1_), custom_call_target="tpu_custom_call" | custom-call | tf_op jit(solution)/shard_map/low_rank_rows/pallas_call | solution.py:219
  5.1 0.0 copy-start.4
  5.1 0.0 copy-start.3
  5.1 0.0 copy-start.1
  5.1 7.9 %all-to-all-start = ((bf16[16,48,128]{2,1,0:T(8,128)(2,1)}), bf16[16,48,128]{2,1,0:T(8,128)(2,1)S(1)}, u32[]{:S(2)}, u32[]{:S(2)}) async-start(bf16[16,48,128]{2,1,0:T(8,128)(2,1)} %low_rank_rows.1), calls=%async_computation | async-start | bytes 393216 | tf_op jit(solution)/shard_map/all_to_all | solution.py:227
  13.1 0.0 copy-done.4
  13.1 2.3 %collective-permute-start.1 = (bf16[64,512]{1,0:T(8,128)(2,1)S(1)}, bf16[64,512]{1,0:T(8,128)(2,1)S(1)}, u32[]{:S(2)}, u32[]{:S(2)}) collective-permute-start(bf16[64,512]{1,0:T(8,128)(2,1)S(1)} %copy-done.4), channel_id=1, source_target_pairs={{0,0},{1,2},{2,4},{3,6},{4,8},{5,10},{6,12},{7,14},{8,16},{9,18},{... | collective-permute-start | bytes 196616 | tf_op jit(solution)/shard_map/ppermute | solution.py:234
  15.4 0.0 copy-done.3
  15.4 2.7 %collective-permute-start.2 = (bf16[64,512]{1,0:T(8,128)(2,1)S(1)}, bf16[64,512]{1,0:T(8,128)(2,1)S(1)}, u32[]{:S(2)}, u32[]{:S(2)}) collective-permute-start(bf16[64,512]{1,0:T(8,128)(2,1)S(1)} %copy-done.3), channel_id=1, source_target_pairs={{0,1},{1,3},{2,5},{3,7},{4,9},{5,11},{6,13},{7,15},{8,17},{9,19},{... | collective-permute-start | bytes 196616 | tf_op jit(solution)/shard_map/ppermute | solution.py:234
  18.1 3.2 %collective-permute-done.1.refs_0_ = bf16[64,512]{1,0:T(8,128)(2,1)S(1)} collective-permute-done((bf16[64,512]{1,0:T(8,128)(2,1)S(1)}, bf16[64,512]{1,0:T(8,128)(2,1)S(1)}, u32[]{:S(2)}, u32[]{:S(2)}) %collective-permute-start.1) | collective-permute-done | bytes 65568 | tf_op jit(solution)/shard_map/ppermute | solution.py:234
  21.2 1.6 %collective-permute-done.2.refs_1_ = bf16[64,512]{1,0:T(8,128)(2,1)S(1)} collective-permute-done((bf16[64,512]{1,0:T(8,128)(2,1)S(1)}, bf16[64,512]{1,0:T(8,128)(2,1)S(1)}, u32[]{:S(2)}, u32[]{:S(2)}) %collective-permute-start.2) | collective-permute-done | bytes 65568 | tf_op jit(solution)/shard_map/ppermute | solution.py:234
  22.8 0.0 all-to-all-done.got_ref
  22.8 0.0 copy-done.1
  22.8 1.0 %owner_outputs.1 = (bf16[32,1024]{1,0:T(8,128)(2,1)}, bf16[32,1024]{1,0:T(8,128)(2,1)}, f32[32,32]{1,0:T(8,128)}, f32[32,32]{1,0:T(8,128)}) custom-call(bf16[16,48,128]{2,1,0:T(8,128)(2,1)S(1)} %all-to-all-done.got_ref, bf16[32,1024]{1,0:T(8,128)(2,1)S(1)} %copy-done.1, bf16[64,512]{1,0:T(8,128)(2,1)S(1)} %collective-permute-done.1.refs_0_, ...), custom_call_target="tpu_custom_call" | custom-call | tf_op jit(solution)/shard_map/owner_outputs/pallas_call | solution.py:236
Async XLA Ops:
  0.6 2.8 %collective-permute-start = (bf16[32,32]{1,0:T(8,128)(2,1)}, bf16[32,32]{1,0:T(8,128)(2,1)S(1)}, u32[]{:S(2)}, u32[]{:S(2)}) collective-permute-start(bf16[32,32]{1,0:T(8,128)(2,1)} %refs_0_.1), channel_id=1, source_target_pairs={{0,16},{16,0},{1,17},{17,1},{2,18},{18,2},{3,19},{19,3},{4,20},{20... | collective-permute-start | bytes 6152 | tf_op jit(solution)/shard_map/ppermute | solution.py:191
  0.9 2.5 %copy-start.2 = (bf16[32,32]{1,0:T(8,128)(2,1)S(1)}, bf16[32,32]{1,0:T(8,128)(2,1)}, u32[]{:S(2)}) copy-start(bf16[32,32]{1,0:T(8,128)(2,1)} %refs_0_.1) | copy-start | bytes 6148
  3.5 0.9 %copy-start = (bf16[16,32,128]{2,1,0:T(8,128)(2,1)S(1)}, bf16[16,32,128]{2,1,0:T(8,128)(2,1)}, u32[]{:S(2)}) copy-start(bf16[16,32,128]{2,1,0:T(8,128)(2,1)} %get-tuple-element.14.both_grad_ref) | copy-start | bytes 393220
  5.1 7.9 %copy-start.4 = (bf16[64,512]{1,0:T(8,128)(2,1)S(1)}, bf16[64,512]{1,0:T(8,128)(2,1)}, u32[]{:S(2)}) copy-start(bf16[64,512]{1,0:T(8,128)(2,1)} %get-tuple-element.15) | copy-start | bytes 196612
  5.1 10.2 %copy-start.3 = (bf16[64,512]{1,0:T(8,128)(2,1)S(1)}, bf16[64,512]{1,0:T(8,128)(2,1)}, u32[]{:S(2)}) copy-start(bf16[64,512]{1,0:T(8,128)(2,1)} %get-tuple-element.16) | copy-start | bytes 196612
  5.1 17.7 %copy-start.1 = (bf16[32,1024]{1,0:T(8,128)(2,1)S(1)}, bf16[32,1024]{1,0:T(8,128)(2,1)}, u32[]{:S(2)}) copy-start(bf16[32,1024]{1,0:T(8,128)(2,1)} %up_ref.1) | copy-start | bytes 196612
  5.1 17.7 %all-to-all-start = ((bf16[16,48,128]{2,1,0:T(8,128)(2,1)}), bf16[16,48,128]{2,1,0:T(8,128)(2,1)S(1)}, u32[]{:S(2)}, u32[]{:S(2)}) async-start(bf16[16,48,128]{2,1,0:T(8,128)(2,1)} %low_rank_rows.1), calls=%async_computation | async-start | bytes 393216 | tf_op jit(solution)/shard_map/all_to_all | solution.py:227
  13.1 8.2 %collective-permute-start.1 = (bf16[64,512]{1,0:T(8,128)(2,1)S(1)}, bf16[64,512]{1,0:T(8,128)(2,1)S(1)}, u32[]{:S(2)}, u32[]{:S(2)}) collective-permute-start(bf16[64,512]{1,0:T(8,128)(2,1)S(1)} %copy-done.4), channel_id=1, source_target_pairs={{0,0},{1,2},{2,4},{3,6},{4,8},{5,10},{6,12},{7,14},{8,16},{9,18},{... | collective-permute-start | bytes 196616 | tf_op jit(solution)/shard_map/ppermute | solution.py:234
  15.4 7.4 %collective-permute-start.2 = (bf16[64,512]{1,0:T(8,128)(2,1)S(1)}, bf16[64,512]{1,0:T(8,128)(2,1)S(1)}, u32[]{:S(2)}, u32[]{:S(2)}) collective-permute-start(bf16[64,512]{1,0:T(8,128)(2,1)S(1)} %copy-done.3), channel_id=1, source_target_pairs={{0,1},{1,3},{2,5},{3,7},{4,9},{5,11},{6,13},{7,15},{8,17},{9,19},{... | collective-permute-start | bytes 196616 | tf_op jit(solution)/shard_map/ppermute | solution.py:234

commit v7 on v6

--- a/solution.py
+++ b/solution.py
@@ -128,9 +128,15 @@
             out_ref[block, rows + group * CUT:rows + (group + 1) * CUT, :] = part
 
 
-def owner_kernel(dp, mp, got_ref, up_ref, *refs):
-    piece_refs = refs[:dp]
-    key_ref, value_ref, low_grad_ref, up_grad_ref = refs[dp:dp + 4]
+def order_kernel(*refs):
+    *arrived_refs, out_ref = refs
+    dp = len(arrived_refs)
+    me = lax.axis_index("dp") * lax.axis_size("mp") + lax.axis_index("mp")
+    for s, arrived_ref in enumerate(arrived_refs):
+        out_ref[lax.rem(lax.rem(me, dp) + dp - s, dp)] = arrived_ref[...]
+
+
+def owner_kernel(dp, mp, got_ref, up_ref, pieces_ref, key_ref, value_ref, low_grad_ref, up_grad_ref):
     rows = key_ref.shape[0]
     both_rank = up_ref.shape[0]
     rank = both_rank // 2
@@ -148,7 +154,6 @@
     column = lax.broadcasted_iota(jnp.int32, from_key.shape, 1)
     low_grad_ref[...] = adapter_factor * jnp.where(column < rank, from_key, from_value)
 
-    me = lax.axis_index("dp") * mp + lax.axis_index("mp")
     side = LANES // both_rank
     cuts = rows // CUT
     half = mp * CUT
@@ -159,14 +164,12 @@
     for group in range(dp * cuts // side):
         at = rows + group * CUT
         lows.append(jnp.concatenate([got_ref[place, at:at + CUT, :] for place in places], axis=0))
-    for s in range(dp):
-        pack = lax.rem(lax.rem(me, dp) + dp - s, dp)
+    for pack in range(dp):
         for cut in range(cuts):
-            piece = piece_refs[s][:, cut * half:(cut + 1) * half]
+            piece = pieces_ref[pack, :, cut * half:(cut + 1) * half]
             slot = pack * cuts + cut
-            for group, low in enumerate(lows):
-                product = jnp.dot(piece, low, preferred_element_type=jnp.float32)
-                total += jnp.where(lane + group * side == slot, product, 0.0)
+            product = jnp.dot(piece, lows[slot // side], preferred_element_type=jnp.float32)
+            total += jnp.where(lane == slot % side, product, 0.0)
     share = total[:, :both_rank]
     for at in range(1, side):
         share += total[:, at * both_rank:(at + 1) * both_rank]
@@ -233,6 +236,18 @@
         route = [(d * mp + h, h * dp + (d + s) % dp) for d in range(dp) for h in range(mp)]
         arrived.append(lax.ppermute(pieces[s], ("dp", "mp"), route))
 
+    pieces = pl.pallas_call(
+        order_kernel,
+        out_shape=jax.ShapeDtypeStruct((dp, 2 * step, src_count), jnp.bfloat16),
+        in_specs=[vmem] * dp,
+        out_specs=vmem,
+        compiler_params=params,
+        cost_estimate=pl.CostEstimate(
+            flops=2 ** 36, bytes_accessed=2 ** 28, transcendentals=0
+        ),
+        name="order_pieces",
+    )(*arrived)
+
     key_gradient, value_grad, low_grad, up_grad = pl.pallas_call(
         functools.partial(owner_kernel, dp, mp),
         out_shape=[
@@ -241,11 +256,11 @@
             jax.ShapeDtypeStruct((rows, both_rank), jnp.float32),
             jax.ShapeDtypeStruct((step, both_rank), jnp.float32),
         ],
-        in_specs=[vmem] * (2 + dp),
+        in_specs=[vmem] * 3,
         out_specs=[vmem] * 4,
         compiler_params=params,
         name="owner_outputs",
-    )(got, adapter_up_matrix, *arrived)
+    )(got, adapter_up_matrix, pieces)
     return query_grad_t.T, key_gradient, value_grad, low_grad, up_grad
 
 

time: 24.1 us -> 29.8 us (1.24)
  the two profiles are of different devices: /device:TPU:7 before, /device:TPU:0 now
where the time goes in v7:
time: 29.8 us; the launch traced here: 29.5 us
  starting transfers between devices  12.4 us (42%)
  waiting for transfers between devices  11.2 us (38%)
  Pallas kernels  4.28 us (14%)
  local copies, waits for them, and re-layouts  0.91 us (3%)
  between operations  0.68 us (2%)
    all_to_all x1, waiting for transfers between devices, local(): lax.all_to_all(sent, 'mp', split_axis=0, concat_axis=0, axis_index_groups...  7.56 us
    all_to_all x1, starting transfers between devices, local(): lax.all_to_all(sent, 'mp', split_axis=0, concat_axis=0, axis_index_groups...  7.37 us
    ppermute x2, starting transfers between devices, local(): arrived.append(lax.ppermute(pieces[s], ('dp', 'mp'), route))  5.03 us
    ppermute x1, waiting for transfers between devices, local(): lax.ppermute(low_rank, 'dp', [(d, (d + s) % dp) for d in range(dp)])  3.64 us
    pallas_call x1, Pallas kernels, local(): pl.pallas_call(functools.partial(attention_kernel, rows), out_shape=[jax....  2.49 us
    pallas_call x1, Pallas kernels, local(): pl.pallas_call(functools.partial(owner_kernel, dp, mp), out_shape=[jax.Sh...  0.99 us
    unnamed x6, local copies, waits for them, and re-layouts  0.91 us
    pallas_call x1, Pallas kernels, local(): pl.pallas_call(functools.partial(low_rank_kernel, rows), out_shape=jax.Sh...  0.77 us
  transfers between devices with their start and end apart: 4, of which 2 were waited for; matrix products, arithmetic and copies ran while one was open for 0% of the time, Pallas kernels for 3%

profile of v7, /device:TPU:0, one launch (start us, length us, event | category | flops | bytes accessed | tf_op | source)
XLA Modules:
  0.0 29.5 jit_solution(15774626341774276599)
XLA Ops:
  0.6 0.0 copy-start.2
  0.6 2.5 %attention_backward.1 = (bf16[64,256]{1,0:T(8,128)(2,1)}, bf16[16,32,128]{2,1,0:T(8,128)(2,1)}, bf16[64,512]{1,0:T(8,128)(2,1)}, bf16[64,512]{1,0:T(8,128)(2,1)}) custom-call(s32[1,8]{1,0:T(1,128)} %source_any.1, s32[1,8]{1,0:T(1,128)} %target_any.1, bf16[64,256]{1,0:T(8,128)(2,1)} %bitcast.3, bf16[64,256]{1,0:T(8,128)(2,1)} %bitcast.4, bf16[512,128]{1,0:T(8,128)(2,1)} %kv_any.1), custom_call_target="tpu_custom_call" | custom-call | flops 167772160 | bytes 8388608 | tf_op jit(solution)/shard_map/attention_backward/pallas_call | solution.py:198
  3.1 1.5 %collective-permute-start.1 = (bf16[64,512]{1,0:T(8,128)(2,1)}, bf16[64,512]{1,0:T(8,128)(2,1)S(1)}, u32[]{:S(2)}, u32[]{:S(2)}) collective-permute-start(bf16[64,512]{1,0:T(8,128)(2,1)} %get-tuple-element.15), channel_id=1, source_target_pairs={{0,0},{1,2},{2,4},{3,6},{4,8},{5,10},{6,12},{7,14},{8,16},{9,18},{... | collective-permute-start | bytes 196616 | tf_op jit(solution)/shard_map/ppermute | solution.py:237
  4.6 3.5 %collective-permute-start.2 = (bf16[64,512]{1,0:T(8,128)(2,1)}, bf16[64,512]{1,0:T(8,128)(2,1)S(1)}, u32[]{:S(2)}, u32[]{:S(2)}) collective-permute-start(bf16[64,512]{1,0:T(8,128)(2,1)} %get-tuple-element.16), channel_id=1, source_target_pairs={{0,1},{1,3},{2,5},{3,7},{4,9},{5,11},{6,13},{7,15},{8,17},{9,19},{... | collective-permute-start | bytes 196616 | tf_op jit(solution)/shard_map/ppermute | solution.py:237
  8.2 0.0 copy-done.2
  8.2 0.0 collective-permute-start
  8.2 3.6 %collective-permute-done.refs_1_ = bf16[32,32]{1,0:T(8,128)(2,1)S(1)} collective-permute-done((bf16[32,32]{1,0:T(8,128)(2,1)S(1)}, bf16[32,32]{1,0:T(8,128)(2,1)S(1)}, u32[]{:S(2)}, u32[]{:S(2)}) %collective-permute-start) | collective-permute-done | bytes 2080 | tf_op jit(solution)/shard_map/ppermute | solution.py:194
  11.8 0.0 copy-start
  11.8 0.9 %copy-done = bf16[16,32,128]{2,1,0:T(8,128)(2,1)S(1)} copy-done((bf16[16,32,128]{2,1,0:T(8,128)(2,1)S(1)}, bf16[16,32,128]{2,1,0:T(8,128)(2,1)}, u32[]{:S(2)}) %copy-start) | copy-done | bytes 131096
  12.7 0.8 %low_rank_rows.1 = bf16[16,48,128]{2,1,0:T(8,128)(2,1)} custom-call(bf16[16,32,128]{2,1,0:T(8,128)(2,1)S(1)} %copy-done, bf16[32,32]{1,0:T(8,128)(2,1)S(1)} %copy-done.2, bf16[32,32]{1,0:T(8,128)(2,1)S(1)} %collective-permute-done.refs_1_), custom_call_target="tpu_custom_call" | custom-call | tf_op jit(solution)/shard_map/low_rank_rows/pallas_call | solution.py:222
  13.5 7.4 %all-to-all-start = ((bf16[16,48,128]{2,1,0:T(8,128)(2,1)}), bf16[16,48,128]{2,1,0:T(8,128)(2,1)S(1)}, u32[]{:S(2)}, u32[]{:S(2)}) async-start(bf16[16,48,128]{2,1,0:T(8,128)(2,1)} %low_rank_rows.1), calls=%async_computation | async-start | bytes 393216 | tf_op jit(solution)/shard_map/all_to_all | solution.py:230
  20.9 0.0 copy-start.1
  20.9 0.0 collective-permute-done.1.refs_0_
  20.9 0.0 collective-permute-done.2.refs_1_
  20.9 7.6 %all-to-all-done.got_ref = bf16[16,48,128]{2,1,0:T(8,128)(2,1)S(1)} async-done(((bf16[16,48,128]{2,1,0:T(8,128)(2,1)}), bf16[16,48,128]{2,1,0:T(8,128)(2,1)S(1)}, u32[]{:S(2)}, u32[]{:S(2)}) %all-to-all-start) | async-done | bytes 196640 | tf_op jit(solution)/shard_map/all_to_all | solution.py:230
  28.5 0.0 copy-done.1
  28.5 1.0 %owner_outputs.1 = (bf16[32,1024]{1,0:T(8,128)(2,1)}, bf16[32,1024]{1,0:T(8,128)(2,1)}, f32[32,32]{1,0:T(8,128)}, f32[32,32]{1,0:T(8,128)}) custom-call(bf16[16,48,128]{2,1,0:T(8,128)(2,1)S(1)} %all-to-all-done.got_ref, bf16[32,1024]{1,0:T(8,128)(2,1)S(1)} %copy-done.1, bf16[2,64,512]{2,1,0:T(8,128)(2,1)S(1)} %order_pieces.1.pieces_ref), custom_call_target="tpu_custom_call" | custom-call | tf_op jit(solution)/shard_map/owner_outputs/pallas_call | solution.py:251
  (1 shorter events, 0.0 us)
Async XLA Ops:
  0.6 7.5 %copy-start.2 = (bf16[32,32]{1,0:T(8,128)(2,1)S(1)}, bf16[32,32]{1,0:T(8,128)(2,1)}, u32[]{:S(2)}) copy-start(bf16[32,32]{1,0:T(8,128)(2,1)} %refs_0_.1) | copy-start | bytes 6148
  3.1 17.7 %collective-permute-start.1 = (bf16[64,512]{1,0:T(8,128)(2,1)}, bf16[64,512]{1,0:T(8,128)(2,1)S(1)}, u32[]{:S(2)}, u32[]{:S(2)}) collective-permute-start(bf16[64,512]{1,0:T(8,128)(2,1)} %get-tuple-element.15), channel_id=1, source_target_pairs={{0,0},{1,2},{2,4},{3,6},{4,8},{5,10},{6,12},{7,14},{8,16},{9,18},{... | collective-permute-start | bytes 196616 | tf_op jit(solution)/shard_map/ppermute | solution.py:237
  4.6 16.2 %collective-permute-start.2 = (bf16[64,512]{1,0:T(8,128)(2,1)}, bf16[64,512]{1,0:T(8,128)(2,1)S(1)}, u32[]{:S(2)}, u32[]{:S(2)}) collective-permute-start(bf16[64,512]{1,0:T(8,128)(2,1)} %get-tuple-element.16), channel_id=1, source_target_pairs={{0,1},{1,3},{2,5},{3,7},{4,9},{5,11},{6,13},{7,15},{8,17},{9,19},{... | collective-permute-start | bytes 196616 | tf_op jit(solution)/shard_map/ppermute | solution.py:237
  8.2 3.7 %collective-permute-start = (bf16[32,32]{1,0:T(8,128)(2,1)S(1)}, bf16[32,32]{1,0:T(8,128)(2,1)S(1)}, u32[]{:S(2)}, u32[]{:S(2)}) collective-permute-start(bf16[32,32]{1,0:T(8,128)(2,1)S(1)} %copy-done.2), channel_id=1, source_target_pairs={{0,16},{16,0},{1,17},{17,1},{2,18},{18,2},{3,19},{19,3},{4,20},{20... | collective-permute-start | bytes 6152 | tf_op jit(solution)/shard_map/ppermute | solution.py:194
  11.8 0.9 %copy-start = (bf16[16,32,128]{2,1,0:T(8,128)(2,1)S(1)}, bf16[16,32,128]{2,1,0:T(8,128)(2,1)}, u32[]{:S(2)}) copy-start(bf16[16,32,128]{2,1,0:T(8,128)(2,1)} %get-tuple-element.14.both_grad_ref) | copy-start | bytes 393220
  13.5 15.0 %all-to-all-start = ((bf16[16,48,128]{2,1,0:T(8,128)(2,1)}), bf16[16,48,128]{2,1,0:T(8,128)(2,1)S(1)}, u32[]{:S(2)}, u32[]{:S(2)}) async-start(bf16[16,48,128]{2,1,0:T(8,128)(2,1)} %low_rank_rows.1), calls=%async_computation | async-start | bytes 393216 | tf_op jit(solution)/shard_map/all_to_all | solution.py:230
  20.9 7.6 %copy-start.1 = (bf16[32,1024]{1,0:T(8,128)(2,1)S(1)}, bf16[32,1024]{1,0:T(8,128)(2,1)}, u32[]{:S(2)}) copy-start(bf16[32,1024]{1,0:T(8,128)(2,1)} %up_ref.1) | copy-start | bytes 196612
